TPU v7x, 32 devices: a whole 2x2x4 slice. The times are simulated.
32 devices in a mesh: lev: 4 (over x, core), hor: 8 (over z, y).
Axes of the slice: x: 2, y: 2, z: 4, core: 2. Of those that a mesh axis runs over, the one named last changes fastest.
Arguments:
- state: float32 [2, 128, 128, 1024], P(None, 'lev', 'hor'), may hold values from -6 to 6
- cotangent: bfloat16 [2, 128, 128, 1024], P(None, 'lev', 'hor'), may hold values from -6 to 6
- diffusion: float32 [128, 128, 1024], P('lev', 'hor'), may hold values from 0.02 to 0.2
- vertical_inverse: float32 [2, 128, 128], replicated, may hold values from -0.2 to 2
- w_in: bfloat16 [1024, 256], replicated, may hold values from -0.375 to 0.375
- w_out: bfloat16 [256, 1024], replicated, may hold values from -0.1875 to 0.1875
Outputs:
- state_adjoint: float32 [2, 128, 128, 1024], P(None, 'lev', 'hor')
All inputs are finite; a program needn't handle non-finite values.
Results may differ from a plain program's by a relative error of at most 0.002.
Values may be sent and summed in bfloat16 or wider, within the bound.
No kernel may reach another device: no remote copies, remote signals or barrier semaphores. Data moves between devices by JAX's collectives and lax.ppermute only.
A program may use at most 64 MiB of HBM per device.

v0:
```python
import functools

import jax
import jax.numpy as jnp
from jax import lax
from jax.experimental import pallas as pl
from jax.experimental.pallas import tpu as pltpu
from jax.sharding import PartitionSpec as P

F32, BF16 = jnp.float32, jnp.bfloat16
VMEM_MIB = 20
PARAMS = pltpu.CompilerParams(vmem_limit_bytes=VMEM_MIB * 1024 * 1024)
COST = pl.CostEstimate(flops=1, bytes_accessed=1, transcendentals=0)
COLUMN_COST = pl.CostEstimate(flops=1, bytes_accessed=3_000_000, transcendentals=0)
VMEM = pl.BlockSpec(memory_space=pltpu.VMEM)
ANY = pl.BlockSpec(memory_space=pl.ANY)
SMEM = pl.BlockSpec(memory_space=pltpu.SMEM)


def row_table(rows, count):
    if count == rows:
        return [list(range(rows))]
    half = rows // 2
    middle = [0, half - 1, half, rows - 1]
    inner = [row for row in range(rows) if row not in middle]
    order = middle + inner
    return [order[c * count : (c + 1) * count] for c in range(rows // count)]


def pick(values, at):
    out = jnp.int32(values[0])
    for i, value in enumerate(values[1:], 1):
        out = jnp.where(at == i, jnp.int32(value), out)
    return out


def in_hbm(x):
    return pltpu.with_memory_space_constraint(x, pltpu.HBM)


def link_type(distance):
    return F32 if distance < 2 else BF16


def lateral(row):
    width = row.shape[1]
    lane = lax.broadcasted_iota(jnp.int32, row.shape, 1)
    left = jnp.where(lane == 0, 0.0, pltpu.roll(row, 1, 1))
    right = jnp.where(lane == width - 1, 0.0, pltpu.roll(row, width - 1, 1))
    return left + right


def dot(a, b):
    return jnp.dot(a, b, preferred_element_type=F32)


def halves(x):
    top = x.astype(BF16)
    return top, (x - top.astype(F32)).astype(BF16)


def by_row(x, rows, wanted, exact):
    levels = x.shape[0] // rows
    level = lax.broadcasted_iota(jnp.int32, (levels, x.shape[0]), 0)
    source = lax.broadcasted_iota(jnp.int32, (levels, x.shape[0]), 1)
    matrix = jnp.concatenate(
        [jnp.where(source == level * rows + row, 1.0, 0.0) for row in wanted], axis=0
    ).astype(BF16)
    if exact:
        out = dot(matrix, x)
    else:
        top, rest = halves(x)
        out = dot(matrix, top) + dot(matrix, rest)
    return {row: out[i * levels : (i + 1) * levels] for i, row in enumerate(wanted)}


def by_level(lines):
    rows, levels = len(lines), lines[0].shape[0]
    size = rows * levels
    target = lax.broadcasted_iota(jnp.int32, (size, levels), 0)
    level = lax.broadcasted_iota(jnp.int32, (size, levels), 1)
    matrix = jnp.concatenate(
        [jnp.where(target == level * rows + row, 1.0, 0.0) for row in range(rows)], axis=1
    ).astype(BF16)
    top, rest = halves(jnp.concatenate(lines, axis=0))
    return dot(jnp.concatenate([matrix, matrix], axis=1), jnp.concatenate([top, rest], axis=0))


def edge_rows_kernel(rows, state_ref, after_ref, first, last):
    lines = by_row(state_ref[...], rows, [0, rows - 1], True)
    first[...] = lines[0].astype(BF16)
    last[...] = lines[rows - 1].astype(BF16)


def edge_rows(state, after):
    fields, levels, rows, width = state.shape
    step = min(levels, 16)
    slab = pl.BlockSpec((None, step, width), lambda i, f: (f, i, 0))
    return pl.pallas_call(
        functools.partial(edge_rows_kernel, rows),
        out_shape=[jax.ShapeDtypeStruct((fields, levels, width), BF16)] * 2,
        grid=(levels // step, fields),
        in_specs=[pl.BlockSpec((None, step * rows, width), lambda i, f: (f, i, 0)), ANY],
        out_specs=[slab] * 2,
        compiler_params=PARAMS,
        cost_estimate=COST,
        name="edge_rows",
    )(in_hbm(state.reshape(fields, levels * rows, width)), after)


def split_kernel(table, count, rows, me_ref, cot_ref, *refs):
    outs, held = refs[: count - 1], refs[-1]
    me = me_ref[0]
    step = held.shape[1]
    here_at = pl.ds(pl.multiple_of(pl.program_id(0) * step, step), step)
    f = pl.program_id(1)
    lines = by_row(cot_ref[...], rows, list(range(rows)), True)
    for r in range(rows):
        held[r] = lines[r]
    for c, order in enumerate(table):
        for k in range(1, count):
            outs[k - 1][c, f, here_at, :] = held[pick(order, me ^ k)].astype(BF16)


def split_cot(me, cot, table, count):
    fields, levels, rows, width = cot.shape
    step = min(levels, 16)
    return pl.pallas_call(
        functools.partial(split_kernel, table, count, rows),
        out_shape=[pltpu.VMEM((len(table), fields, levels, width), BF16)] * (count - 1),
        grid=(levels // step, fields),
        in_specs=[SMEM, pl.BlockSpec((None, step * rows, width), lambda i, f: (f, i, 0))],
        out_specs=[VMEM] * (count - 1),
        scratch_shapes=[pltpu.VMEM((rows, step, width), F32)],
        compiler_params=PARAMS,
        cost_estimate=COST,
        name="split_cot",
    )(me, in_hbm(cot.reshape(fields, levels * rows, width)))


def transpose_kernel(v_ref, win_ref, wout_ref, after_ref, vt_ref, wint_ref, woutt_ref):
    for f in range(v_ref.shape[0]):
        vt_ref[f] = v_ref[f].T
    wint_ref[...] = win_ref[...].T
    woutt_ref[...] = wout_ref[...].T


def transposes(v, w_in, w_out, after):
    shapes = [(v.shape, F32), (w_in.shape[::-1], BF16), (w_out.shape[::-1], BF16)]
    return pl.pallas_call(
        transpose_kernel,
        out_shape=[pltpu.VMEM(dims, kind) for dims, kind in shapes],
        in_specs=[VMEM] * 3 + [ANY],
        out_specs=[VMEM] * 3,
        compiler_params=PARAMS,
        cost_estimate=COST,
        name="transposes",
    )(v, w_in, w_out, after)


def release_kernel(count, *refs):
    for source, target in zip(refs[:count], refs[-count:]):
        target[...] = source[...]


def release(pieces, after):
    return pl.pallas_call(
        functools.partial(release_kernel, len(pieces)),
        out_shape=[pltpu.VMEM(x.shape, x.dtype) for x in pieces],
        in_specs=[VMEM] * len(pieces) + [ANY] * len(after),
        out_specs=[VMEM] * len(pieces),
        compiler_params=PARAMS,
        cost_estimate=COST,
        name="release",
    )(*pieces, *after)


def forward_kernel(table, count, rows, me_ref, cot_ref, state_ref, diff_ref, low_ref, high_ref, *refs):
    own, diff_rows, *far, cot_rows, rows_held = refs[2:]
    me = me_ref[0]
    step = rows_held.shape[1]
    here_at = pl.ds(pl.multiple_of(pl.program_id(0) * step, step), step)
    f = pl.program_id(1)
    every = list(range(rows))
    lines = by_row(state_ref[...], rows, every, False)
    lines[-1] = low_ref[f, here_at, :].astype(F32)
    lines[rows] = high_ref[f, here_at, :].astype(F32)

    @pl.when(f == 0)
    def _():
        diff = by_row(diff_ref[...], rows, every, False)
        for r in every:
            diff_rows[r, here_at, :] = diff[r]

    cots = by_row(cot_ref[...], rows, every, True)
    for r in every:
        here = lines[r]
        total = lines[r - 1] + lines[r + 1] + lateral(here) - 4.0 * here
        rows_held[r] = here + diff_rows[r, here_at, :] * total
        cot_rows[r] = cots[r]
    for c, order in enumerate(table):
        for k in range(count):
            row = pick(order, me ^ k)
            if k == 0:
                own[c, 0, f, here_at, :] = cot_rows[row]
                own[c, 1, f, here_at, :] = rows_held[row]
            else:
                out = far[c * (count - 1) + k - 1]
                out[f, here_at, :] = rows_held[row].astype(out.dtype)


def forward(me, cot, state, diffusion, low, high, after, table, count):
    fields, levels, rows, width = state.shape
    step = min(levels, 16)
    chunks = len(table)
    shape = (fields, levels, width)
    outs = [(F32, (chunks, 2, *shape)), (F32, (rows, levels, width))]
    outs += [(link_type(k), shape) for _ in table for k in range(1, count)]
    tile = pl.BlockSpec((None, step * rows, width), lambda i, f: (f, i, 0))
    own, diff, *far = pl.pallas_call(
        functools.partial(forward_kernel, table, count, rows),
        out_shape=[pltpu.VMEM(dims, kind) for kind, dims in outs],
        grid=(levels // step, fields),
        in_specs=[SMEM, tile, tile]
        + [pl.BlockSpec((step * rows, width), lambda i, f: (i, 0))]
        + [VMEM] * 2
        + [ANY] * 2,
        out_specs=[VMEM] * len(outs),
        scratch_shapes=[pltpu.VMEM((rows, step, width), F32)] * 2,
        compiler_params=PARAMS,
        cost_estimate=COST,
        name="forward",
    )(
        me,
        in_hbm(cot.reshape(fields, levels * rows, width)),
        in_hbm(state.reshape(fields, levels * rows, width)),
        in_hbm(diffusion.reshape(levels * rows, width)),
        low,
        high,
        *after,
    )
    return own, diff, [far[c * (count - 1) : (c + 1) * (count - 1)] for c in range(chunks)]


def vertical(matrix, x):
    m_top, m_rest = halves(matrix)
    x_top, x_rest = halves(x)
    return dot(m_top, x_top) + (dot(m_rest, x_top) + dot(m_top, x_rest))


def column_kernel(count, at, tile, me_ref, own, *refs):
    far_cot, far = refs[: count - 1], refs[count - 1 : 2 * count - 2]
    v_ref, vt_ref, win_ref, wint_ref, woutt_ref = refs[2 * count - 2 : 2 * count + 3]
    outs, (cols, cot_cols, back) = refs[-count - 3 : -3], refs[-3:]
    fields, lev, _ = v_ref.shape
    me = me_ref[0]
    levels = lev // count
    lanes = pl.ds(pl.multiple_of(pl.program_id(0) * tile, tile), tile)
    for k in range(count):
        to = pl.ds(pl.multiple_of((me ^ k) * levels, levels), levels)
        for f in range(fields):
            if k == 0:
                cot, diffused = own[at, 0, f, :, lanes], own[at, 1, f, :, lanes]
            else:
                cot, diffused = far_cot[k - 1][at, f, :, lanes], far[k - 1][f, :, lanes]
            cot_cols[f, to, :] = cot.astype(F32)
            cols[f, to, :] = diffused.astype(F32)
    inputs = jnp.concatenate(
        [vertical(v_ref[f], cols[f]).astype(BF16) for f in range(fields)], axis=0
    )
    cot = jnp.concatenate([cot_cols[f] for f in range(fields)], axis=0)
    cot_half = cot.astype(BF16)
    hidden, block = win_ref.shape[0], 256
    grad = cot
    for h in range(0, hidden, block):
        preact = dot(win_ref[h : h + block, :], inputs)
        hidden_grad = dot(woutt_ref[h : h + block, :], cot_half)
        s = 0.5 + 0.5 * jnp.tanh(0.5 * preact)
        pre_grad = (hidden_grad * s * (1.0 + preact * (1.0 - s))).astype(BF16)
        grad = grad + dot(wint_ref[:, h : h + block], pre_grad)
    for f in range(fields):
        back[f] = vertical(vt_ref[f], grad[f * lev : (f + 1) * lev])
    for k in range(count):
        to = pl.ds(pl.multiple_of((me ^ k) * levels, levels), levels)
        for f in range(fields):
            outs[k][f, :, lanes] = back[f, to, :].astype(outs[k].dtype)


def columns(me, own, far_cot, far, at, v, vt, w_in, w_in_t, w_out_t, after, name):
    count = len(far) + 1
    *_, fields, levels, width = own.shape
    lev = v.shape[1]
    tile = min(width, 512)
    inputs = (own, *far_cot, *far, v, vt, w_in, w_in_t, w_out_t)
    return pl.pallas_call(
        functools.partial(column_kernel, count, at, tile),
        out_shape=[pltpu.VMEM((fields, levels, width), link_type(k)) for k in range(count)],
        grid=(width // tile,),
        in_specs=[SMEM] + [VMEM] * len(inputs) + [ANY] * len(after),
        out_specs=[VMEM] * count,
        scratch_shapes=[pltpu.VMEM((fields, lev, tile), F32)] * 3,
        compiler_params=PARAMS,
        cost_estimate=COST,
        name=name,
    )(me, *inputs, *after)


def edge_kernel(order, count, rows, me_ref, diff_ref, *refs):
    pieces, low, high = refs[:count], refs[count], refs[count + 1]
    me = me_ref[0]
    for k in range(count):
        row = pick(order, me ^ k)

        @pl.when(row == 0)
        def _():
            for f in range(low.shape[0]):
                low[f] = (diff_ref[0] * pieces[k][f].astype(F32)).astype(BF16)

        @pl.when(row == rows - 1)
        def _():
            for f in range(low.shape[0]):
                high[f] = (diff_ref[rows - 1] * pieces[k][f].astype(F32)).astype(BF16)


def edges(me, diff, pieces, order):
    rows, levels, width = diff.shape
    shape = pieces[0].shape
    return pl.pallas_call(
        functools.partial(edge_kernel, order, len(pieces), rows),
        out_shape=[pltpu.VMEM(shape, BF16)] * 2,
        in_specs=[SMEM] + [VMEM] * (1 + len(pieces)),
        out_specs=[VMEM] * 2,
        compiler_params=PARAMS,
        cost_estimate=COST,
        name="edges",
    )(me, diff, *pieces)


def final_kernel(table, count, rows, top, me_ref, diff_ref, low_ref, high_ref, pieces, out, held):
    me = me_ref[0]
    step, span, _ = out.shape
    start = top * span
    i, f = pl.program_id(0), pl.program_id(1)
    here_at = pl.ds(pl.multiple_of(i * step, step), step)
    for c, order in enumerate(table):
        for k in range(count):
            held[pick(order, me ^ k)] = pieces[c * count + k][f, here_at, :].astype(F32)

    def weighted(r):
        if r < 0:
            return low_ref[f, here_at, :].astype(F32)
        if r == rows:
            return high_ref[f, here_at, :].astype(F32)
        return held[r] * diff_ref[r, here_at, :]

    lines = []
    before, here = weighted(start - 1), weighted(start)
    for r in range(start, start + span):
        after = weighted(r + 1)
        lines.append(held[r] + before + after + lateral(here) - 4.0 * here)
        before, here = here, after
    out[...] = by_level(lines).reshape(out.shape)


def final(me, diff, low, high, pieces, table, top, base):
    count = len(pieces[0])
    fields, levels, width = low.shape
    rows = diff.shape[0]
    span = rows // 2
    step = min(levels, 16)
    needed = [piece for chunk in pieces for piece in chunk]
    aliased = [] if base is None else [base]

    def kernel(*refs):
        final_kernel(
            table[: len(pieces)], count, rows, top, *refs[:4], refs[4 : 4 + len(needed)], *refs[-2:]
        )

    return pl.pallas_call(
        kernel,
        out_shape=pltpu.HBM((fields, levels, rows, width), F32),
        grid=(levels // step, fields),
        in_specs=[SMEM] + [VMEM] * (3 + len(needed)) + [ANY] * len(aliased),
        out_specs=pl.BlockSpec((None, step, span, width), lambda i, f: (f, i, top, 0)),
        scratch_shapes=[pltpu.VMEM((rows, step, width), F32)],
        input_output_aliases={4 + len(needed): 0} if aliased else {},
        compiler_params=PARAMS,
        cost_estimate=COST,
        name=f"final_{top}",
    )(me, diff, low, high, *needed, *aliased)


def swap(x, distance, count):
    if distance == 0:
        return x
    return lax.ppermute(x, "lev", [(i, i ^ distance) for i in range(count)])


def halo(first, last):
    count = lax.axis_size("hor")
    forward = [(i, i + 1) for i in range(count - 1)]
    backward = [(target, source) for source, target in forward]
    return lax.ppermute(last, "hor", forward), lax.ppermute(first, "hor", backward)


def body(state, cotangent, diffusion, vertical_inverse, w_in, w_out):
    count = lax.axis_size("lev")
    rows = state.shape[2]
    table = row_table(rows, count)
    chunks = len(table)
    me = lax.axis_index("lev").astype(jnp.int32).reshape(1)
    split = split_cot(me, cotangent, table, count)
    far_cot = [swap(x, k, count) for k, x in enumerate(split, 1)]
    edge = edge_rows(state, split[0])
    low, high = halo(*edge)
    v_t, w_in_t, w_out_t = transposes(vertical_inverse, w_in, w_out, edge[0])
    weights = (vertical_inverse, v_t, w_in, w_in_t, w_out_t)
    after = [far_cot[0], w_in_t]
    own, diff, far = forward(me, cotangent, state, diffusion, low, high, after, table, count)
    returned, last = [], []

    def send(pieces):
        return [swap(x, k, count) for k, x in enumerate(pieces, 1)]

    moved = [send(pieces) for pieces in far[:2]]
    for c in range(chunks):
        if c + 2 < chunks:
            ready = release(far[c + 2], moved[c] + last)
            moved.append(send(ready))
            last = [ready[0]]
        out = columns(me, own, far_cot, moved[c], c, *weights, last, f"columns_{c}")
        last = [out[0]]
        returned.append([out[0]] + send(out[1:]))
    chunk_of = {row: c for c, order in enumerate(table) for row in order}
    edge = chunk_of[0]
    low, high = halo(*edges(me, diff, returned[edge], table[edge]))
    span = rows // 2
    needed = 1 + max(chunk_of[row] for row in range(span + 1))
    result = final(me, diff, low, high, returned[:needed], table, 0, None)
    return final(me, diff, low, high, returned, table, 1, result)


def solution(mesh):
    placed = (
        P(None, "lev", "hor", None),
        P(None, "lev", "hor", None),
        P("lev", "hor", None),
        P(),
        P(),
        P(),
    )
    return jax.shard_map(
        body, mesh=mesh, in_specs=placed, out_specs=P(None, "lev", "hor", None), check_vma=False
    )
```

profile of v0, /device:TPU:25, one launch (start us, length us, event | category | flops | bytes accessed | tf_op | source)
XLA Modules:
  0.0 98.1 jit_solution(2319662354284448732)
XLA Ops:
  0.0 3.3 %split_cot.1 = (bf16[4,2,32,1024]{3,2,1,0:T(8,128)(2,1)S(1)}, bf16[4,2,32,1024]{3,2,1,0:T(8,128)(2,1)S(1)}, bf16[4,2,32,1024]{3,2,1,0:T(8,128)(2,1)S(1)}) custom-call(s32[1]{0:T(128)} %bitcast.me_ref.refs_0_, bf16[2,512,1024]{2,1,0:T(8,128)(2,1)} %bitcast.6), custom_call_target="tpu_custom_call" | custom-call | flops 1 | bytes 1 | tf_op jit(solution)/shard_map/split_cot/pallas_call | solution.py:128
  4.0 1.2 %collective-permute-start.3 = (bf16[4,2,32,1024]{3,2,1,0:T(8,128)(2,1)S(1)}, bf16[4,2,32,1024]{3,2,1,0:T(8,128)(2,1)S(1)}, u32[]{:S(2)}, u32[]{:S(2)}) collective-permute-start(bf16[4,2,32,1024]{3,2,1,0:T(8,128)(2,1)S(1)} %get-tuple-element.57), channel_id=1, source_target_pairs={{0,16},{8,24},{16,0},{24,8},{1,17},{9,25},{17,1},{25,9},{2,18},{10... | collective-permute-start | bytes 1572872 | tf_op jit(solution)/shard_map/ppermute | solution.py:396
  5.8 3.3 %edge_rows.1 = (bf16[2,32,1024]{2,1,0:T(8,128)(2,1)S(1)}, bf16[2,32,1024]{2,1,0:T(8,128)(2,1)S(1)}) custom-call(f32[2,512,1024]{2,1,0:T(8,128)} %bitcast.4, bf16[4,2,32,1024]{3,2,1,0:T(8,128)(2,1)S(1)} %get-tuple-element.51.after_ref), custom_call_target="tpu_custom_call" | custom-call | flops 1 | bytes 1 | tf_op jit(solution)/shard_map/edge_rows/pallas_call | solution.py:99
  9.1 3.1 %collective-permute-start = (bf16[2,32,1024]{2,1,0:T(8,128)(2,1)S(1)}, bf16[2,32,1024]{2,1,0:T(8,128)(2,1)S(1)}, u32[]{:S(2)}, u32[]{:S(2)}) collective-permute-start(bf16[2,32,1024]{2,1,0:T(8,128)(2,1)S(1)} %get-tuple-element.52), channel_id=1, source_target_pairs={{0,1},{1,2},{2,3},{3,4},{4,5},{5,6},{6,7},{8,9},{9,10},{10,11},{11... | collective-permute-start | bytes 393224 | tf_op jit(solution)/shard_map/ppermute | solution.py:403
  12.2 3.0 %collective-permute-start.1 = (bf16[2,32,1024]{2,1,0:T(8,128)(2,1)S(1)}, bf16[2,32,1024]{2,1,0:T(8,128)(2,1)S(1)}, u32[]{:S(2)}, u32[]{:S(2)}) collective-permute-start(bf16[2,32,1024]{2,1,0:T(8,128)(2,1)S(1)} %get-tuple-element.53.after_ref), channel_id=1, source_target_pairs={{1,0},{2,1},{3,2},{4,3},{5,4},{6,5},{7,6},{9,8},{10,9},{11,10},{12... | collective-permute-start | bytes 393224 | tf_op jit(solution)/shard_map/ppermute | solution.py:403
  16.8 3.0 %collective-permute-done.1.high_ref = bf16[2,32,1024]{2,1,0:T(8,128)(2,1)S(1)} collective-permute-done((bf16[2,32,1024]{2,1,0:T(8,128)(2,1)S(1)}, bf16[2,32,1024]{2,1,0:T(8,128)(2,1)S(1)}, u32[]{:S(2)}, u32[]{:S(2)}) %collective-permute-start.1) | collective-permute-done | bytes 131104 | tf_op jit(solution)/shard_map/ppermute | solution.py:403
  19.9 8.5 %forward.1 = (f32[4,2,2,32,1024]{4,3,2,1,0:T(8,128)S(1)}, f32[16,32,1024]{2,1,0:T(8,128)S(1)}, f32[2,32,1024]{2,1,0:T(8,128)S(1)}, bf16[2,32,1024]{2,1,0:T(8,128...) custom-call(s32[1]{0:T(128)} %bitcast.me_ref.refs_0_, ...), custom_call_target="tpu_custom_call" | custom-call | flops 1 | bytes 1 | tf_op jit(solution)/shard_map/forward/pallas_call | solution.py:220
  29.1 1.3 %collective-permute-start.6 = (bf16[2,32,1024]{2,1,0:T(8,128)(2,1)S(1)}, bf16[2,32,1024]{2,1,0:T(8,128)(2,1)S(1)}, u32[]{:S(2)}, u32[]{:S(2)}) collective-permute-start(bf16[2,32,1024]{2,1,0:T(8,128)(2,1)S(1)} %get-tuple-element.60), channel_id=1, source_target_pairs={{0,16},{8,24},{16,0},{24,8},{1,17},{9,25},{17,1},{25,9},{2,18},{10... | collective-permute-start | bytes 393224 | tf_op jit(solution)/shard_map/ppermute | solution.py:396
  30.9 3.4 %collective-permute-done.6.refs_4_ = bf16[2,32,1024]{2,1,0:T(8,128)(2,1)S(1)} collective-permute-done((bf16[2,32,1024]{2,1,0:T(8,128)(2,1)S(1)}, bf16[2,32,1024]{2,1,0:T(8,128)(2,1)S(1)}, u32[]{:S(2)}, u32[]{:S(2)}) %collective-permute-start.6) | collective-permute-done | bytes 131104 | tf_op jit(solution)/shard_map/ppermute | solution.py:396
  34.2 1.3 %collective-permute-start.13 = (f32[2,32,1024]{2,1,0:T(8,128)S(1)}, f32[2,32,1024]{2,1,0:T(8,128)S(1)}, u32[]{:S(2)}, u32[]{:S(2)}) collective-permute-start(f32[2,32,1024]{2,1,0:T(8,128)S(1)} %get-tuple-element.74), channel_id=1, source_target_pairs={{0,8},{8,0},{16,24},{24,16},{1,9},{9,1},{17,25},{25,17},{2,10},{10... | collective-permute-start | bytes 786440 | tf_op jit(solution)/shard_map/ppermute | solution.py:396
  35.5 1.7 %collective-permute-done.7.refs_5_ = bf16[2,32,1024]{2,1,0:T(8,128)(2,1)S(1)} collective-permute-done((bf16[2,32,1024]{2,1,0:T(8,128)(2,1)S(1)}, bf16[2,32,1024]{2,1,0:T(8,128)(2,1)S(1)}, u32[]{:S(2)}, u32[]{:S(2)}) %collective-permute-start.7) | collective-permute-done | bytes 131104 | tf_op jit(solution)/shard_map/ppermute | solution.py:396
  37.2 1.2 %collective-permute-start.14 = (bf16[2,32,1024]{2,1,0:T(8,128)(2,1)S(1)}, bf16[2,32,1024]{2,1,0:T(8,128)(2,1)S(1)}, u32[]{:S(2)}, u32[]{:S(2)}) collective-permute-start(bf16[2,32,1024]{2,1,0:T(8,128)(2,1)S(1)} %get-tuple-element.75), channel_id=1, source_target_pairs={{0,16},{8,24},{16,0},{24,8},{1,17},{9,25},{17,1},{25,9},{2,18},{10... | collective-permute-start | bytes 393224 | tf_op jit(solution)/shard_map/ppermute | solution.py:396
  39.1 1.3 %collective-permute-start.20 = (bf16[2,32,1024]{2,1,0:T(8,128)(2,1)S(1)}, bf16[2,32,1024]{2,1,0:T(8,128)(2,1)S(1)}, u32[]{:S(2)}, u32[]{:S(2)}) collective-permute-start(bf16[2,32,1024]{2,1,0:T(8,128)(2,1)S(1)} %get-tuple-element.85), channel_id=1, source_target_pairs={{0,16},{8,24},{16,0},{24,8},{1,17},{9,25},{17,1},{25,9},{2,18},{10... | collective-permute-start | bytes 393224 | tf_op jit(solution)/shard_map/ppermute | solution.py:396
  40.8 5.0 %columns_0.1 = (f32[2,32,1024]{2,1,0:T(8,128)S(1)}, f32[2,32,1024]{2,1,0:T(8,128)S(1)}, bf16[2,32,1024]{2,1,0:T(8,128)(2,1)S(1)}, bf16[2,32,1024]{2,1,0:T(8,128)(2,1)S(1)}) custom-call(s32[1]{0:T(128)} %bitcast.me_ref.refs_0_, f32[4,2,2,32,1024]{4,3,2,1,0:T(8,128)S(1)} %get-tuple-element.56.own, bf16[4,2,32,1024]{3,2,1,0:T(8,128)(2,1)S(1)} %collective-permute-done.2.refs_0_, ...), custom_call_target="tpu_custom_call" | custom-call | flops 1 | bytes 1 | tf_op jit(solution)/shard_map/columns_0/pallas_call | solution.py:295
  45.8 1.3 %collective-permute-start.9 = (bf16[2,32,1024]{2,1,0:T(8,128)(2,1)S(1)}, bf16[2,32,1024]{2,1,0:T(8,128)(2,1)S(1)}, u32[]{:S(2)}, u32[]{:S(2)}) collective-permute-start(bf16[2,32,1024]{2,1,0:T(8,128)(2,1)S(1)} %get-tuple-element.70), channel_id=1, source_target_pairs={{0,16},{8,24},{16,0},{24,8},{1,17},{9,25},{17,1},{25,9},{2,18},{10... | collective-permute-start | bytes 393224 | tf_op jit(solution)/shard_map/ppermute | solution.py:396
  47.7 2.8 %collective-permute-start.10 = (bf16[2,32,1024]{2,1,0:T(8,128)(2,1)S(1)}, bf16[2,32,1024]{2,1,0:T(8,128)(2,1)S(1)}, u32[]{:S(2)}, u32[]{:S(2)}) collective-permute-start(bf16[2,32,1024]{2,1,0:T(8,128)(2,1)S(1)} %get-tuple-element.71), channel_id=1, source_target_pairs={{0,24},{8,16},{16,8},{24,0},{1,25},{9,17},{17,9},{25,1},{2,26},{10... | collective-permute-start | bytes 393224 | tf_op jit(solution)/shard_map/ppermute | solution.py:396
  51.5 1.2 %collective-permute-start.26 = (bf16[2,32,1024]{2,1,0:T(8,128)(2,1)S(1)}, bf16[2,32,1024]{2,1,0:T(8,128)(2,1)S(1)}, u32[]{:S(2)}, u32[]{:S(2)}) collective-permute-start(bf16[2,32,1024]{2,1,0:T(8,128)(2,1)S(1)} %get-tuple-element.91), channel_id=1, source_target_pairs={{0,16},{8,24},{16,0},{24,8},{1,17},{9,25},{17,1},{25,9},{2,18},{10... | collective-permute-start | bytes 393224 | tf_op jit(solution)/shard_map/ppermute | solution.py:396
  53.3 1.7 %collective-permute-start.25 = (f32[2,32,1024]{2,1,0:T(8,128)S(1)}, f32[2,32,1024]{2,1,0:T(8,128)S(1)}, u32[]{:S(2)}, u32[]{:S(2)}) collective-permute-start(f32[2,32,1024]{2,1,0:T(8,128)S(1)} %get-tuple-element.80.refs_11_), channel_id=1, source_target_pairs={{0,8},{8,0},{16,24},{24,16},{1,9},{9,1},{17,25},{25,17},{2,10},{10... | collective-permute-start | bytes 786440 | tf_op jit(solution)/shard_map/ppermute | solution.py:396
  55.0 5.0 %columns_1.1 = (f32[2,32,1024]{2,1,0:T(8,128)S(1)}, f32[2,32,1024]{2,1,0:T(8,128)S(1)}, bf16[2,32,1024]{2,1,0:T(8,128)(2,1)S(1)}, bf16[2,32,1024]{2,1,0:T(8,128)(2,1)S(1)}) custom-call(s32[1]{0:T(128)} %bitcast.me_ref.refs_0_, f32[4,2,2,32,1024]{4,3,2,1,0:T(8,128)S(1)} %get-tuple-element.56.own, bf16[4,2,32,1024]{3,2,1,0:T(8,128)(2,1)S(1)} %collective-permute-done.2.refs_0_, ...), custom_call_target="tpu_custom_call" | custom-call | flops 1 | bytes 1 | tf_op jit(solution)/shard_map/columns_1/pallas_call | solution.py:295
  60.1 1.6 %collective-permute-start.27 = (bf16[2,32,1024]{2,1,0:T(8,128)(2,1)S(1)}, bf16[2,32,1024]{2,1,0:T(8,128)(2,1)S(1)}, u32[]{:S(2)}, u32[]{:S(2)}) collective-permute-start(bf16[2,32,1024]{2,1,0:T(8,128)(2,1)S(1)} %get-tuple-element.92), channel_id=1, source_target_pairs={{0,24},{8,16},{16,8},{24,0},{1,25},{9,17},{17,9},{25,1},{2,26},{10... | collective-permute-start | bytes 393224 | tf_op jit(solution)/shard_map/ppermute | solution.py:396
  61.9 1.5 %collective-permute-start.18 = (bf16[2,32,1024]{2,1,0:T(8,128)(2,1)S(1)}, bf16[2,32,1024]{2,1,0:T(8,128)(2,1)S(1)}, u32[]{:S(2)}, u32[]{:S(2)}) collective-permute-start(bf16[2,32,1024]{2,1,0:T(8,128)(2,1)S(1)} %get-tuple-element.84), channel_id=1, source_target_pairs={{0,24},{8,16},{16,8},{24,0},{1,25},{9,17},{17,9},{25,1},{2,26},{10... | collective-permute-start | bytes 393224 | tf_op jit(solution)/shard_map/ppermute | solution.py:396
  63.5 5.0 %columns_2.1 = (f32[2,32,1024]{2,1,0:T(8,128)S(1)}, f32[2,32,1024]{2,1,0:T(8,128)S(1)}, bf16[2,32,1024]{2,1,0:T(8,128)(2,1)S(1)}, bf16[2,32,1024]{2,1,0:T(8,128)(2,1)S(1)}) custom-call(s32[1]{0:T(128)} %bitcast.me_ref.refs_0_, f32[4,2,2,32,1024]{4,3,2,1,0:T(8,128)S(1)} %get-tuple-element.56.own, bf16[4,2,32,1024]{3,2,1,0:T(8,128)(2,1)S(1)} %collective-permute-done.2.refs_0_, ...), custom_call_target="tpu_custom_call" | custom-call | flops 1 | bytes 1 | tf_op jit(solution)/shard_map/columns_2/pallas_call | solution.py:295
  68.5 1.9 %collective-permute-start.11 = (bf16[2,32,1024]{2,1,0:T(8,128)(2,1)S(1)}, bf16[2,32,1024]{2,1,0:T(8,128)(2,1)S(1)}, u32[]{:S(2)}, u32[]{:S(2)}) collective-permute-start(bf16[2,32,1024]{2,1,0:T(8,128)(2,1)S(1)} %get-tuple-element.72), channel_id=1, source_target_pairs={{0,1},{1,2},{2,3},{3,4},{4,5},{5,6},{6,7},{8,9},{9,10},{10,11},{11... | collective-permute-start | bytes 393224 | tf_op jit(solution)/shard_map/ppermute | solution.py:403
  70.4 4.4 %collective-permute-start.12 = (bf16[2,32,1024]{2,1,0:T(8,128)(2,1)S(1)}, bf16[2,32,1024]{2,1,0:T(8,128)(2,1)S(1)}, u32[]{:S(2)}, u32[]{:S(2)}) collective-permute-start(bf16[2,32,1024]{2,1,0:T(8,128)(2,1)S(1)} %get-tuple-element.73), channel_id=1, source_target_pairs={{1,0},{2,1},{3,2},{4,3},{5,4},{6,5},{7,6},{9,8},{10,9},{11,10},{12... | collective-permute-start | bytes 393224 | tf_op jit(solution)/shard_map/ppermute | solution.py:403
  74.9 5.0 %columns_3.1 = (f32[2,32,1024]{2,1,0:T(8,128)S(1)}, f32[2,32,1024]{2,1,0:T(8,128)S(1)}, bf16[2,32,1024]{2,1,0:T(8,128)(2,1)S(1)}, bf16[2,32,1024]{2,1,0:T(8,128)(2,1)S(1)}) custom-call(s32[1]{0:T(128)} %bitcast.me_ref.refs_0_, f32[4,2,2,32,1024]{4,3,2,1,0:T(8,128)S(1)} %get-tuple-element.56.own, bf16[4,2,32,1024]{3,2,1,0:T(8,128)(2,1)S(1)} %collective-permute-done.2.refs_0_, ...), custom_call_target="tpu_custom_call" | custom-call | flops 1 | bytes 1 | tf_op jit(solution)/shard_map/columns_3/pallas_call | solution.py:295
  81.3 1.3 %collective-permute-start.24 = (bf16[2,32,1024]{2,1,0:T(8,128)(2,1)S(1)}, bf16[2,32,1024]{2,1,0:T(8,128)(2,1)S(1)}, u32[]{:S(2)}, u32[]{:S(2)}) collective-permute-start(bf16[2,32,1024]{2,1,0:T(8,128)(2,1)S(1)} %get-tuple-element.90), channel_id=1, source_target_pairs={{0,24},{8,16},{16,8},{24,0},{1,25},{9,17},{17,9},{25,1},{2,26},{10... | collective-permute-start | bytes 393224 | tf_op jit(solution)/shard_map/ppermute | solution.py:396
  82.8 3.0 %collective-permute-done.23.refs_14_ = bf16[2,32,1024]{2,1,0:T(8,128)(2,1)S(1)} collective-permute-done((bf16[2,32,1024]{2,1,0:T(8,128)(2,1)S(1)}, bf16[2,32,1024]{2,1,0:T(8,128)(2,1)S(1)}, u32[]{:S(2)}, u32[]{:S(2)}) %collective-permute-start.23) | collective-permute-done | bytes 131104 | tf_op jit(solution)/shard_map/ppermute | solution.py:396
  85.8 1.4 %collective-permute-start.30 = (bf16[2,32,1024]{2,1,0:T(8,128)(2,1)S(1)}, bf16[2,32,1024]{2,1,0:T(8,128)(2,1)S(1)}, u32[]{:S(2)}, u32[]{:S(2)}) collective-permute-start(bf16[2,32,1024]{2,1,0:T(8,128)(2,1)S(1)} %get-tuple-element.96), channel_id=1, source_target_pairs={{0,24},{8,16},{16,8},{24,0},{1,25},{9,17},{17,9},{25,1},{2,26},{10... | collective-permute-start | bytes 393224 | tf_op jit(solution)/shard_map/ppermute | solution.py:396
  87.2 2.0 %collective-permute-done.24.refs_15_ = bf16[2,32,1024]{2,1,0:T(8,128)(2,1)S(1)} collective-permute-done((bf16[2,32,1024]{2,1,0:T(8,128)(2,1)S(1)}, bf16[2,32,1024]{2,1,0:T(8,128)(2,1)S(1)}, u32[]{:S(2)}, u32[]{:S(2)}) %collective-permute-start.24) | collective-permute-done | bytes 131104 | tf_op jit(solution)/shard_map/ppermute | solution.py:396
  89.2 3.7 %final_0.1.refs_20_ = f32[2,32,16,1024]{3,2,1,0:T(8,128)} custom-call(s32[1]{0:T(128)} %bitcast.me_ref.refs_0_, f32[16,32,1024]{2,1,0:T(8,128)S(1)} %get-tuple-element.55.diff_ref.refs_1_, bf16[2,32,1024]{2,1,0:T(8,128)(2,1)S(1)} %collective-permute-done.11.refs_2_, bf16[2,32,1024]{2,1,0:T(8,128)(2,1)S(1)} %collective-permute-done.12.refs_3_, ...), custom_call_target="tpu_custom_call" | custom-call | flops 1 | bytes 1 | tf_op jit(solution)/shard_map/final_0/pallas_call | solution.py:379
  92.9 1.5 %collective-permute-done.30.refs_19_ = bf16[2,32,1024]{2,1,0:T(8,128)(2,1)S(1)} collective-permute-done((bf16[2,32,1024]{2,1,0:T(8,128)(2,1)S(1)}, bf16[2,32,1024]{2,1,0:T(8,128)(2,1)S(1)}, u32[]{:S(2)}, u32[]{:S(2)}) %collective-permute-start.30) | collective-permute-done | bytes 131104 | tf_op jit(solution)/shard_map/ppermute | solution.py:396
  94.4 3.7 %final_1.1 = f32[2,32,16,1024]{3,2,1,0:T(8,128)} custom-call(s32[1]{0:T(128)} %bitcast.me_ref.refs_0_, f32[16,32,1024]{2,1,0:T(8,128)S(1)} %get-tuple-element.55.diff_ref.refs_1_, bf16[2,32,1024]{2,1,0:T(8,128)(2,1)S(1)} %collective-permute-done.11.refs_2_, ...), custom_call_target="tpu_custom_call", output_to_operand_aliasing={{}: (20, {})} | custom-call | flops 1 | bytes 1 | tf_op jit(solution)/shard_map/final_1/pallas_call | solution.py:379
  (49 shorter events, 9.2 us)
Async XLA Ops:
  3.3 16.6 %collective-permute-start.2 = (bf16[4,2,32,1024]{3,2,1,0:T(8,128)(2,1)S(1)}, bf16[4,2,32,1024]{3,2,1,0:T(8,128)(2,1)S(1)}, u32[]{:S(2)}, u32[]{:S(2)}) collective-permute-start(bf16[4,2,32,1024]{3,2,1,0:T(8,128)(2,1)S(1)} %get-tuple-element.51.after_ref), channel_id=1, source_target_pairs={{0,8},{8,0},{16,24},{24,16},{1,9},{9,1},{17,25},{25,17},{2,10},{10... | collective-permute-start | bytes 1572872 | tf_op jit(solution)/shard_map/ppermute | solution.py:396
  4.0 35.1 %collective-permute-start.3 = (bf16[4,2,32,1024]{3,2,1,0:T(8,128)(2,1)S(1)}, bf16[4,2,32,1024]{3,2,1,0:T(8,128)(2,1)S(1)}, u32[]{:S(2)}, u32[]{:S(2)}) collective-permute-start(bf16[4,2,32,1024]{3,2,1,0:T(8,128)(2,1)S(1)} %get-tuple-element.57), channel_id=1, source_target_pairs={{0,16},{8,24},{16,0},{24,8},{1,17},{9,25},{17,1},{25,9},{2,18},{10... | collective-permute-start | bytes 1572872 | tf_op jit(solution)/shard_map/ppermute | solution.py:396
  5.3 35.1 %collective-permute-start.4 = (bf16[4,2,32,1024]{3,2,1,0:T(8,128)(2,1)S(1)}, bf16[4,2,32,1024]{3,2,1,0:T(8,128)(2,1)S(1)}, u32[]{:S(2)}, u32[]{:S(2)}) collective-permute-start(bf16[4,2,32,1024]{3,2,1,0:T(8,128)(2,1)S(1)} %get-tuple-element.58), channel_id=1, source_target_pairs={{0,24},{8,16},{16,8},{24,0},{1,25},{9,17},{17,9},{25,1},{2,26},{10... | collective-permute-start | bytes 1572872 | tf_op jit(solution)/shard_map/ppermute | solution.py:396
  5.8 9.6 %copy-start.2 = (bf16[256,1024]{1,0:T(8,128)(2,1)S(1)}, bf16[256,1024]{1,0:T(8,128)(2,1)}, u32[]{:S(2)}) copy-start(bf16[256,1024]{1,0:T(8,128)(2,1)} %wout_ref.1) | copy-start | bytes 1572868
  9.1 7.7 %collective-permute-start = (bf16[2,32,1024]{2,1,0:T(8,128)(2,1)S(1)}, bf16[2,32,1024]{2,1,0:T(8,128)(2,1)S(1)}, u32[]{:S(2)}, u32[]{:S(2)}) collective-permute-start(bf16[2,32,1024]{2,1,0:T(8,128)(2,1)S(1)} %get-tuple-element.52), channel_id=1, source_target_pairs={{0,1},{1,2},{2,3},{3,4},{4,5},{5,6},{6,7},{8,9},{9,10},{10,11},{11... | collective-permute-start | bytes 393224 | tf_op jit(solution)/shard_map/ppermute | solution.py:403
  12.2 7.6 %collective-permute-start.1 = (bf16[2,32,1024]{2,1,0:T(8,128)(2,1)S(1)}, bf16[2,32,1024]{2,1,0:T(8,128)(2,1)S(1)}, u32[]{:S(2)}, u32[]{:S(2)}) collective-permute-start(bf16[2,32,1024]{2,1,0:T(8,128)(2,1)S(1)} %get-tuple-element.53.after_ref), channel_id=1, source_target_pairs={{1,0},{2,1},{3,2},{4,3},{5,4},{6,5},{7,6},{9,8},{10,9},{11,10},{12... | collective-permute-start | bytes 393224 | tf_op jit(solution)/shard_map/ppermute | solution.py:403
  28.3 10.1 %collective-permute-start.5 = (f32[2,32,1024]{2,1,0:T(8,128)S(1)}, f32[2,32,1024]{2,1,0:T(8,128)S(1)}, u32[]{:S(2)}, u32[]{:S(2)}) collective-permute-start(f32[2,32,1024]{2,1,0:T(8,128)S(1)} %get-tuple-element.59), channel_id=1, source_target_pairs={{0,8},{8,0},{16,24},{24,16},{1,9},{9,1},{17,25},{25,17},{2,10},{10... | collective-permute-start | bytes 786440 | tf_op jit(solution)/shard_map/ppermute | solution.py:396
  29.1 5.1 %collective-permute-start.6 = (bf16[2,32,1024]{2,1,0:T(8,128)(2,1)S(1)}, bf16[2,32,1024]{2,1,0:T(8,128)(2,1)S(1)}, u32[]{:S(2)}, u32[]{:S(2)}) collective-permute-start(bf16[2,32,1024]{2,1,0:T(8,128)(2,1)S(1)} %get-tuple-element.60), channel_id=1, source_target_pairs={{0,16},{8,24},{16,0},{24,8},{1,17},{9,25},{17,1},{25,9},{2,18},{10... | collective-permute-start | bytes 393224 | tf_op jit(solution)/shard_map/ppermute | solution.py:396
  30.4 6.8 %collective-permute-start.7 = (bf16[2,32,1024]{2,1,0:T(8,128)(2,1)S(1)}, bf16[2,32,1024]{2,1,0:T(8,128)(2,1)S(1)}, u32[]{:S(2)}, u32[]{:S(2)}) collective-permute-start(bf16[2,32,1024]{2,1,0:T(8,128)(2,1)S(1)} %get-tuple-element.61), channel_id=1, source_target_pairs={{0,24},{8,16},{16,8},{24,0},{1,25},{9,17},{17,9},{25,1},{2,26},{10... | collective-permute-start | bytes 393224 | tf_op jit(solution)/shard_map/ppermute | solution.py:396
  34.2 13.4 %collective-permute-start.13 = (f32[2,32,1024]{2,1,0:T(8,128)S(1)}, f32[2,32,1024]{2,1,0:T(8,128)S(1)}, u32[]{:S(2)}, u32[]{:S(2)}) collective-permute-start(f32[2,32,1024]{2,1,0:T(8,128)S(1)} %get-tuple-element.74), channel_id=1, source_target_pairs={{0,8},{8,0},{16,24},{24,16},{1,9},{9,1},{17,25},{25,17},{2,10},{10... | collective-permute-start | bytes 786440 | tf_op jit(solution)/shard_map/ppermute | solution.py:396
  37.2 8.6 %collective-permute-start.14 = (bf16[2,32,1024]{2,1,0:T(8,128)(2,1)S(1)}, bf16[2,32,1024]{2,1,0:T(8,128)(2,1)S(1)}, u32[]{:S(2)}, u32[]{:S(2)}) collective-permute-start(bf16[2,32,1024]{2,1,0:T(8,128)(2,1)S(1)} %get-tuple-element.75), channel_id=1, source_target_pairs={{0,16},{8,24},{16,0},{24,8},{1,17},{9,25},{17,1},{25,9},{2,18},{10... | collective-permute-start | bytes 393224 | tf_op jit(solution)/shard_map/ppermute | solution.py:396
  38.4 8.7 %collective-permute-start.15 = (bf16[2,32,1024]{2,1,0:T(8,128)(2,1)S(1)}, bf16[2,32,1024]{2,1,0:T(8,128)(2,1)S(1)}, u32[]{:S(2)}, u32[]{:S(2)}) collective-permute-start(bf16[2,32,1024]{2,1,0:T(8,128)(2,1)S(1)} %get-tuple-element.76), channel_id=1, source_target_pairs={{0,24},{8,16},{16,8},{24,0},{1,25},{9,17},{17,9},{25,1},{2,26},{10... | collective-permute-start | bytes 393224 | tf_op jit(solution)/shard_map/ppermute | solution.py:396
  39.1 8.6 %collective-permute-start.20 = (bf16[2,32,1024]{2,1,0:T(8,128)(2,1)S(1)}, bf16[2,32,1024]{2,1,0:T(8,128)(2,1)S(1)}, u32[]{:S(2)}, u32[]{:S(2)}) collective-permute-start(bf16[2,32,1024]{2,1,0:T(8,128)(2,1)S(1)} %get-tuple-element.85), channel_id=1, source_target_pairs={{0,16},{8,24},{16,0},{24,8},{1,17},{9,25},{17,1},{25,9},{2,18},{10... | collective-permute-start | bytes 393224 | tf_op jit(solution)/shard_map/ppermute | solution.py:396
  40.4 11.1 %collective-permute-start.21 = (bf16[2,32,1024]{2,1,0:T(8,128)(2,1)S(1)}, bf16[2,32,1024]{2,1,0:T(8,128)(2,1)S(1)}, u32[]{:S(2)}, u32[]{:S(2)}) collective-permute-start(bf16[2,32,1024]{2,1,0:T(8,128)(2,1)S(1)} %get-tuple-element.86), channel_id=1, source_target_pairs={{0,24},{8,16},{16,8},{24,0},{1,25},{9,17},{17,9},{25,1},{2,26},{10... | collective-permute-start | bytes 393224 | tf_op jit(solution)/shard_map/ppermute | solution.py:396
  45.8 7.5 %collective-permute-start.9 = (bf16[2,32,1024]{2,1,0:T(8,128)(2,1)S(1)}, bf16[2,32,1024]{2,1,0:T(8,128)(2,1)S(1)}, u32[]{:S(2)}, u32[]{:S(2)}) collective-permute-start(bf16[2,32,1024]{2,1,0:T(8,128)(2,1)S(1)} %get-tuple-element.70), channel_id=1, source_target_pairs={{0,16},{8,24},{16,0},{24,8},{1,17},{9,25},{17,1},{25,9},{2,18},{10... | collective-permute-start | bytes 393224 | tf_op jit(solution)/shard_map/ppermute | solution.py:396
  47.1 14.6 %collective-permute-start.8 = (f32[2,32,1024]{2,1,0:T(8,128)S(1)}, f32[2,32,1024]{2,1,0:T(8,128)S(1)}, u32[]{:S(2)}, u32[]{:S(2)}) collective-permute-start(f32[2,32,1024]{2,1,0:T(8,128)S(1)} %get-tuple-element.69), channel_id=1, source_target_pairs={{0,8},{8,0},{16,24},{24,16},{1,9},{9,1},{17,25},{25,17},{2,10},{10... | collective-permute-start | bytes 786440 | tf_op jit(solution)/shard_map/ppermute | solution.py:396
  47.6 14.3 %collective-permute-start.19 = (f32[2,32,1024]{2,1,0:T(8,128)S(1)}, f32[2,32,1024]{2,1,0:T(8,128)S(1)}, u32[]{:S(2)}, u32[]{:S(2)}) collective-permute-start(f32[2,32,1024]{2,1,0:T(8,128)S(1)} %get-tuple-element.67.refs_11_), channel_id=1, source_target_pairs={{0,8},{8,0},{16,24},{24,16},{1,9},{9,1},{17,25},{25,17},{2,10},{10... | collective-permute-start | bytes 786440 | tf_op jit(solution)/shard_map/ppermute | solution.py:396
  47.7 12.3 %collective-permute-start.10 = (bf16[2,32,1024]{2,1,0:T(8,128)(2,1)S(1)}, bf16[2,32,1024]{2,1,0:T(8,128)(2,1)S(1)}, u32[]{:S(2)}, u32[]{:S(2)}) collective-permute-start(bf16[2,32,1024]{2,1,0:T(8,128)(2,1)S(1)} %get-tuple-element.71), channel_id=1, source_target_pairs={{0,24},{8,16},{16,8},{24,0},{1,25},{9,17},{17,9},{25,1},{2,26},{10... | collective-permute-start | bytes 393224 | tf_op jit(solution)/shard_map/ppermute | solution.py:396
  51.5 8.6 %collective-permute-start.26 = (bf16[2,32,1024]{2,1,0:T(8,128)(2,1)S(1)}, bf16[2,32,1024]{2,1,0:T(8,128)(2,1)S(1)}, u32[]{:S(2)}, u32[]{:S(2)}) collective-permute-start(bf16[2,32,1024]{2,1,0:T(8,128)(2,1)S(1)} %get-tuple-element.91), channel_id=1, source_target_pairs={{0,16},{8,24},{16,0},{24,8},{1,17},{9,25},{17,1},{25,9},{2,18},{10... | collective-permute-start | bytes 393224 | tf_op jit(solution)/shard_map/ppermute | solution.py:396
  53.3 17.1 %collective-permute-start.25 = (f32[2,32,1024]{2,1,0:T(8,128)S(1)}, f32[2,32,1024]{2,1,0:T(8,128)S(1)}, u32[]{:S(2)}, u32[]{:S(2)}) collective-permute-start(f32[2,32,1024]{2,1,0:T(8,128)S(1)} %get-tuple-element.80.refs_11_), channel_id=1, source_target_pairs={{0,8},{8,0},{16,24},{24,16},{1,9},{9,1},{17,25},{25,17},{2,10},{10... | collective-permute-start | bytes 786440 | tf_op jit(solution)/shard_map/ppermute | solution.py:396
  60.0 21.0 %collective-permute-start.16 = (f32[2,32,1024]{2,1,0:T(8,128)S(1)}, f32[2,32,1024]{2,1,0:T(8,128)S(1)}, u32[]{:S(2)}, u32[]{:S(2)}) collective-permute-start(f32[2,32,1024]{2,1,0:T(8,128)S(1)} %get-tuple-element.82), channel_id=1, source_target_pairs={{0,8},{8,0},{16,24},{24,16},{1,9},{9,1},{17,25},{25,17},{2,10},{10... | collective-permute-start | bytes 786440 | tf_op jit(solution)/shard_map/ppermute | solution.py:396
  60.1 8.4 %collective-permute-start.27 = (bf16[2,32,1024]{2,1,0:T(8,128)(2,1)S(1)}, bf16[2,32,1024]{2,1,0:T(8,128)(2,1)S(1)}, u32[]{:S(2)}, u32[]{:S(2)}) collective-permute-start(bf16[2,32,1024]{2,1,0:T(8,128)(2,1)S(1)} %get-tuple-element.92), channel_id=1, source_target_pairs={{0,24},{8,16},{16,8},{24,0},{1,25},{9,17},{17,9},{25,1},{2,26},{10... | collective-permute-start | bytes 393224 | tf_op jit(solution)/shard_map/ppermute | solution.py:396
  61.7 18.2 %collective-permute-start.17 = (bf16[2,32,1024]{2,1,0:T(8,128)(2,1)S(1)}, bf16[2,32,1024]{2,1,0:T(8,128)(2,1)S(1)}, u32[]{:S(2)}, u32[]{:S(2)}) collective-permute-start(bf16[2,32,1024]{2,1,0:T(8,128)(2,1)S(1)} %get-tuple-element.83), channel_id=1, source_target_pairs={{0,16},{8,24},{16,0},{24,8},{1,17},{9,25},{17,1},{25,9},{2,18},{10... | collective-permute-start | bytes 393224 | tf_op jit(solution)/shard_map/ppermute | solution.py:396
  61.9 18.8 %collective-permute-start.18 = (bf16[2,32,1024]{2,1,0:T(8,128)(2,1)S(1)}, bf16[2,32,1024]{2,1,0:T(8,128)(2,1)S(1)}, u32[]{:S(2)}, u32[]{:S(2)}) collective-permute-start(bf16[2,32,1024]{2,1,0:T(8,128)(2,1)S(1)} %get-tuple-element.84), channel_id=1, source_target_pairs={{0,24},{8,16},{16,8},{24,0},{1,25},{9,17},{17,9},{25,1},{2,26},{10... | collective-permute-start | bytes 393224 | tf_op jit(solution)/shard_map/ppermute | solution.py:396
  68.5 12.8 %collective-permute-start.11 = (bf16[2,32,1024]{2,1,0:T(8,128)(2,1)S(1)}, bf16[2,32,1024]{2,1,0:T(8,128)(2,1)S(1)}, u32[]{:S(2)}, u32[]{:S(2)}) collective-permute-start(bf16[2,32,1024]{2,1,0:T(8,128)(2,1)S(1)} %get-tuple-element.72), channel_id=1, source_target_pairs={{0,1},{1,2},{2,3},{3,4},{4,5},{5,6},{6,7},{8,9},{9,10},{10,11},{11... | collective-permute-start | bytes 393224 | tf_op jit(solution)/shard_map/ppermute | solution.py:403
  70.4 12.2 %collective-permute-start.12 = (bf16[2,32,1024]{2,1,0:T(8,128)(2,1)S(1)}, bf16[2,32,1024]{2,1,0:T(8,128)(2,1)S(1)}, u32[]{:S(2)}, u32[]{:S(2)}) collective-permute-start(bf16[2,32,1024]{2,1,0:T(8,128)(2,1)S(1)} %get-tuple-element.73), channel_id=1, source_target_pairs={{1,0},{2,1},{3,2},{4,3},{5,4},{6,5},{7,6},{9,8},{10,9},{11,10},{12... | collective-permute-start | bytes 393224 | tf_op jit(solution)/shard_map/ppermute | solution.py:403
  79.9 9.3 %collective-permute-start.22 = (f32[2,32,1024]{2,1,0:T(8,128)S(1)}, f32[2,32,1024]{2,1,0:T(8,128)S(1)}, u32[]{:S(2)}, u32[]{:S(2)}) collective-permute-start(f32[2,32,1024]{2,1,0:T(8,128)S(1)} %get-tuple-element.88), channel_id=1, source_target_pairs={{0,8},{8,0},{16,24},{24,16},{1,9},{9,1},{17,25},{25,17},{2,10},{10... | collective-permute-start | bytes 786440 | tf_op jit(solution)/shard_map/ppermute | solution.py:396
  80.7 5.1 %collective-permute-start.23 = (bf16[2,32,1024]{2,1,0:T(8,128)(2,1)S(1)}, bf16[2,32,1024]{2,1,0:T(8,128)(2,1)S(1)}, u32[]{:S(2)}, u32[]{:S(2)}) collective-permute-start(bf16[2,32,1024]{2,1,0:T(8,128)(2,1)S(1)} %get-tuple-element.89), channel_id=1, source_target_pairs={{0,16},{8,24},{16,0},{24,8},{1,17},{9,25},{17,1},{25,9},{2,18},{10... | collective-permute-start | bytes 393224 | tf_op jit(solution)/shard_map/ppermute | solution.py:396
  81.0 13.4 %collective-permute-start.28 = (f32[2,32,1024]{2,1,0:T(8,128)S(1)}, f32[2,32,1024]{2,1,0:T(8,128)S(1)}, u32[]{:S(2)}, u32[]{:S(2)}) collective-permute-start(f32[2,32,1024]{2,1,0:T(8,128)S(1)} %get-tuple-element.94), channel_id=1, source_target_pairs={{0,8},{8,0},{16,24},{24,16},{1,9},{9,1},{17,25},{25,17},{2,10},{10... | collective-permute-start | bytes 786440 | tf_op jit(solution)/shard_map/ppermute | solution.py:396
  81.3 7.9 %collective-permute-start.24 = (bf16[2,32,1024]{2,1,0:T(8,128)(2,1)S(1)}, bf16[2,32,1024]{2,1,0:T(8,128)(2,1)S(1)}, u32[]{:S(2)}, u32[]{:S(2)}) collective-permute-start(bf16[2,32,1024]{2,1,0:T(8,128)(2,1)S(1)} %get-tuple-element.90), channel_id=1, source_target_pairs={{0,24},{8,16},{16,8},{24,0},{1,25},{9,17},{17,9},{25,1},{2,26},{10... | collective-permute-start | bytes 393224 | tf_op jit(solution)/shard_map/ppermute | solution.py:396
  82.6 10.3 %collective-permute-start.29 = (bf16[2,32,1024]{2,1,0:T(8,128)(2,1)S(1)}, bf16[2,32,1024]{2,1,0:T(8,128)(2,1)S(1)}, u32[]{:S(2)}, u32[]{:S(2)}) collective-permute-start(bf16[2,32,1024]{2,1,0:T(8,128)(2,1)S(1)} %get-tuple-element.95), channel_id=1, source_target_pairs={{0,16},{8,24},{16,0},{24,8},{1,17},{9,25},{17,1},{25,9},{2,18},{10... | collective-permute-start | bytes 393224 | tf_op jit(solution)/shard_map/ppermute | solution.py:396
  85.8 8.6 %collective-permute-start.30 = (bf16[2,32,1024]{2,1,0:T(8,128)(2,1)S(1)}, bf16[2,32,1024]{2,1,0:T(8,128)(2,1)S(1)}, u32[]{:S(2)}, u32[]{:S(2)}) collective-permute-start(bf16[2,32,1024]{2,1,0:T(8,128)(2,1)S(1)} %get-tuple-element.96), channel_id=1, source_target_pairs={{0,24},{8,16},{16,8},{24,0},{1,25},{9,17},{17,9},{25,1},{2,26},{10... | collective-permute-start | bytes 393224 | tf_op jit(solution)/shard_map/ppermute | solution.py:396
  (2 other events, 19.1 us)
where the time goes:
time: 98.4 us; the launch traced here: 98.1 us
  Pallas kernels  42.9 us (44%)
  starting transfers between devices  37.7 us (38%)
  waiting for transfers between devices  17.2 us (17%)
    ppermute x27, starting transfers between devices, swap(): return lax.ppermute(x, 'lev', [(i, i ^ distance) for i in range(count)])  25.2 us
    pallas_call x4, Pallas kernels, columns(): pl.pallas_call(functools.partial(column_kernel, count, at, tile), out_sha...  20 us
    ppermute x27, waiting for transfers between devices, swap(): return lax.ppermute(x, 'lev', [(i, i ^ distance) for i in range(count)])  13.1 us
    pallas_call x1, Pallas kernels, forward(): pl.pallas_call(functools.partial(forward_kernel, table, count, rows), out...  8.46 us
    ppermute x2, starting transfers between devices, halo(): lax.ppermute(first, 'hor', backward)  7.47 us
    pallas_call x2, Pallas kernels, final(): pl.pallas_call(kernel, out_shape=pltpu.HBM((fields, levels, rows, width),...  7.35 us
    ppermute x2, starting transfers between devices, halo(): lax.ppermute(last, 'hor', forward)  5.07 us
    pallas_call x1, Pallas kernels, edge_rows(): pl.pallas_call(functools.partial(edge_rows_kernel, rows), out_shape=[jax....  3.32 us
  transfers between devices with their start and end apart: 31, of which 9 were waited for; matrix products, arithmetic and copies ran while one was open for 0% of the time, Pallas kernels for 37%

commit v1 on v0

--- a/solution.py
+++ b/solution.py
@@ -11,7 +11,8 @@
 VMEM_MIB = 20
 PARAMS = pltpu.CompilerParams(vmem_limit_bytes=VMEM_MIB * 1024 * 1024)
 COST = pl.CostEstimate(flops=1, bytes_accessed=1, transcendentals=0)
-COLUMN_COST = pl.CostEstimate(flops=1, bytes_accessed=3_000_000, transcendentals=0)
+COLUMN_COST = pl.CostEstimate(flops=6_000_000_000, bytes_accessed=1, transcendentals=0)
+COLUMN_COST = pl.CostEstimate(flops=6_000_000_000, bytes_accessed=3_000_000, transcendentals=0)
 VMEM = pl.BlockSpec(memory_space=pltpu.VMEM)
 ANY = pl.BlockSpec(memory_space=pl.ANY)
 SMEM = pl.BlockSpec(memory_space=pltpu.SMEM)
@@ -36,6 +37,10 @@
 
 def in_hbm(x):
     return pltpu.with_memory_space_constraint(x, pltpu.HBM)
+
+
+def views(refs, pieces):
+    return [ref if at is None else ref.at[at] for ref, (_, at) in zip(refs, pieces)]
 
 
 def link_type(distance):
@@ -158,33 +163,38 @@
     )(v, w_in, w_out, after)
 
 
-def release_kernel(count, *refs):
-    for source, target in zip(refs[:count], refs[-count:]):
+def release_kernel(stacked, count, *refs):
+    outs = refs[-count - bool(stacked) :]
+    if stacked:
+        outs = [outs[0].at[i] for i in range(stacked)] + list(outs[1:])
+    for source, target in zip(refs, outs):
         target[...] = source[...]
 
 
-def release(pieces, after):
-    return pl.pallas_call(
-        functools.partial(release_kernel, len(pieces)),
-        out_shape=[pltpu.VMEM(x.shape, x.dtype) for x in pieces],
-        in_specs=[VMEM] * len(pieces) + [ANY] * len(after),
-        out_specs=[VMEM] * len(pieces),
+def release(stack, pieces, after):
+    shapes = [(x.shape, x.dtype) for x in pieces]
+    if stack:
+        shapes = [((len(stack), *stack[0].shape), stack[0].dtype)] + shapes
+    return pl.pallas_call(
+        functools.partial(release_kernel, len(stack), len(pieces)),
+        out_shape=[pltpu.VMEM(*shape) for shape in shapes],
+        in_specs=[VMEM] * (len(stack) + len(pieces)) + [ANY] * len(after),
+        out_specs=[VMEM] * len(shapes),
         compiler_params=PARAMS,
         cost_estimate=COST,
         name="release",
-    )(*pieces, *after)
-
-
-def forward_kernel(table, count, rows, me_ref, cot_ref, state_ref, diff_ref, low_ref, high_ref, *refs):
-    own, diff_rows, *far, cot_rows, rows_held = refs[2:]
+    )(*stack, *pieces, *after)
+
+
+def forward_kernel(table, count, rows, me_ref, cot_ref, state_ref, diff_ref, *refs):
+    own_cot, diff_rows, edge, *out, cot_rows, rows_held = refs[1:]
     me = me_ref[0]
     step = rows_held.shape[1]
     here_at = pl.ds(pl.multiple_of(pl.program_id(0) * step, step), step)
     f = pl.program_id(1)
     every = list(range(rows))
     lines = by_row(state_ref[...], rows, every, False)
-    lines[-1] = low_ref[f, here_at, :].astype(F32)
-    lines[rows] = high_ref[f, here_at, :].astype(F32)
+    lines[-1] = lines[rows] = jnp.zeros_like(lines[0])
 
     @pl.when(f == 0)
     def _():
@@ -198,33 +208,28 @@
         total = lines[r - 1] + lines[r + 1] + lateral(here) - 4.0 * here
         rows_held[r] = here + diff_rows[r, here_at, :] * total
         cot_rows[r] = cots[r]
+    for j, r in enumerate(table[0]):
+        edge[j, f, here_at, :] = rows_held[r]
     for c, order in enumerate(table):
-        for k in range(count):
-            row = pick(order, me ^ k)
-            if k == 0:
-                own[c, 0, f, here_at, :] = cot_rows[row]
-                own[c, 1, f, here_at, :] = rows_held[row]
-            else:
-                out = far[c * (count - 1) + k - 1]
-                out[f, here_at, :] = rows_held[row].astype(out.dtype)
-
-
-def forward(me, cot, state, diffusion, low, high, after, table, count):
+        own_cot[c, f, here_at, :] = cot_rows[pick(order, me)]
+        for k in range(count if c else 0):
+            to = out[(c - 1) * count + k]
+            to[f, here_at, :] = rows_held[pick(order, me ^ k)].astype(to.dtype)
+
+
+def forward(me, cot, state, diffusion, after, table, count):
     fields, levels, rows, width = state.shape
     step = min(levels, 16)
     chunks = len(table)
     shape = (fields, levels, width)
-    outs = [(F32, (chunks, 2, *shape)), (F32, (rows, levels, width))]
-    outs += [(link_type(k), shape) for _ in table for k in range(1, count)]
+    outs = [(F32, (chunks, *shape)), (F32, (rows, levels, width)), (F32, (count, *shape))]
+    outs += [(link_type(k), shape) for _ in table[1:] for k in range(count)]
     tile = pl.BlockSpec((None, step * rows, width), lambda i, f: (f, i, 0))
-    own, diff, *far = pl.pallas_call(
+    own_cot, diff, edge, *out = pl.pallas_call(
         functools.partial(forward_kernel, table, count, rows),
         out_shape=[pltpu.VMEM(dims, kind) for kind, dims in outs],
         grid=(levels // step, fields),
-        in_specs=[SMEM, tile, tile]
-        + [pl.BlockSpec((step * rows, width), lambda i, f: (i, 0))]
-        + [VMEM] * 2
-        + [ANY] * 2,
+        in_specs=[SMEM, tile, tile, pl.BlockSpec((step * rows, width), lambda i, f: (i, 0)), ANY],
         out_specs=[VMEM] * len(outs),
         scratch_shapes=[pltpu.VMEM((rows, step, width), F32)] * 2,
         compiler_params=PARAMS,
@@ -235,11 +240,38 @@
         in_hbm(cot.reshape(fields, levels * rows, width)),
         in_hbm(state.reshape(fields, levels * rows, width)),
         in_hbm(diffusion.reshape(levels * rows, width)),
-        low,
-        high,
-        *after,
+        after,
     )
-    return own, diff, [far[c * (count - 1) : (c + 1) * (count - 1)] for c in range(chunks)]
+    return own_cot, diff, edge, [out[c * count : (c + 1) * count] for c in range(chunks - 1)]
+
+
+def halo_kernel(order, rows, others, me_ref, edge_ref, diff_ref, low_ref, high_ref, *refs):
+    outs = list(refs[-len(order) :])
+    me = me_ref[0]
+    for k in range(1, len(order)):
+        if others:
+            outs[k][1] = refs[k - 1][...]
+        outs[k] = outs[k].at[0]
+    for f in range(low_ref.shape[0]):
+        low = diff_ref[0] * low_ref[f].astype(F32)
+        high = diff_ref[rows - 1] * high_ref[f].astype(F32)
+        for k, out in enumerate(outs):
+            row = pick(order, me ^ k)
+            term = jnp.where(row == 0, low, jnp.where(row == rows - 1, high, 0.0))
+            out[f] = (edge_ref[me ^ k, f] + term).astype(out.dtype)
+
+
+def add_halo(me, edge, diff, low, high, others, after, order):
+    shapes = [low.shape] + [(1 + bool(others), *low.shape)] * (len(order) - 1)
+    return pl.pallas_call(
+        functools.partial(halo_kernel, order, diff.shape[0], bool(others)),
+        out_shape=[pltpu.VMEM(dims, link_type(k)) for k, dims in enumerate(shapes)],
+        in_specs=[SMEM] + [VMEM] * (4 + len(others)) + [ANY] * len(after),
+        out_specs=[VMEM] * len(order),
+        compiler_params=PARAMS,
+        cost_estimate=COST,
+        name="add_halo",
+    )(me, edge, diff, low, high, *others, *after)
 
 
 def vertical(matrix, x):
@@ -248,9 +280,9 @@
     return dot(m_top, x_top) + (dot(m_rest, x_top) + dot(m_top, x_rest))
 
 
-def column_kernel(count, at, tile, me_ref, own, *refs):
-    far_cot, far = refs[: count - 1], refs[count - 1 : 2 * count - 2]
-    v_ref, vt_ref, win_ref, wint_ref, woutt_ref = refs[2 * count - 2 : 2 * count + 3]
+def column_kernel(count, at, tile, paired, places, me_ref, own_cot, *refs):
+    far_cot, states = refs[: count - 1], views(refs[count - 1 : 2 * count - 1], places)
+    v_ref, vt_ref, win_ref, wint_ref, woutt_ref = refs[2 * count - 1 : 2 * count + 4]
     outs, (cols, cot_cols, back) = refs[-count - 3 : -3], refs[-3:]
     fields, lev, _ = v_ref.shape
     me = me_ref[0]
@@ -259,12 +291,9 @@
     for k in range(count):
         to = pl.ds(pl.multiple_of((me ^ k) * levels, levels), levels)
         for f in range(fields):
-            if k == 0:
-                cot, diffused = own[at, 0, f, :, lanes], own[at, 1, f, :, lanes]
-            else:
-                cot, diffused = far_cot[k - 1][at, f, :, lanes], far[k - 1][f, :, lanes]
+            cot = (far_cot[k - 1] if k else own_cot)[at, f, :, lanes]
             cot_cols[f, to, :] = cot.astype(F32)
-            cols[f, to, :] = diffused.astype(F32)
+            cols[f, to, :] = states[k][f, :, lanes].astype(F32)
     inputs = jnp.concatenate(
         [vertical(v_ref[f], cols[f]).astype(BF16) for f in range(fields)], axis=0
     )
@@ -283,30 +312,40 @@
     for k in range(count):
         to = pl.ds(pl.multiple_of((me ^ k) * levels, levels), levels)
         for f in range(fields):
-            outs[k][f, :, lanes] = back[f, to, :].astype(outs[k].dtype)
-
-
-def columns(me, own, far_cot, far, at, v, vt, w_in, w_in_t, w_out_t, after, name):
-    count = len(far) + 1
-    *_, fields, levels, width = own.shape
+            value = back[f, to, :].astype(outs[k].dtype)
+            if k == 1:
+                outs[k][len(paired), f, :, lanes] = value
+                for ref in paired:
+                    outs[k][0, f, :, lanes] = refs[ref][0, f, :, lanes]
+            else:
+                outs[k][f, :, lanes] = value
+
+
+def columns(me, own_cot, far_cot, states, at, v, vt, w_in, w_in_t, w_out_t, earlier, after, name):
+    count = len(states)
+    fields, levels, width = states[0][0].shape
     lev = v.shape[1]
     tile = min(width, 512)
-    inputs = (own, *far_cot, *far, v, vt, w_in, w_in_t, w_out_t)
-    return pl.pallas_call(
-        functools.partial(column_kernel, count, at, tile),
-        out_shape=[pltpu.VMEM((fields, levels, width), link_type(k)) for k in range(count)],
+    inputs = (own_cot, *far_cot, *[array for array, _ in states], v, vt, w_in, w_in_t, w_out_t, *earlier)
+    shapes = [(fields, levels, width)] * count
+    shapes[1] = (1 + len(earlier), *shapes[1])
+    paired = [len(inputs) - 2] if earlier else []
+    return pl.pallas_call(
+        functools.partial(column_kernel, count, at, tile, paired, [(None, place) for _, place in states]),
+        out_shape=[pltpu.VMEM(dims, link_type(k)) for k, dims in enumerate(shapes)],
         grid=(width // tile,),
         in_specs=[SMEM] + [VMEM] * len(inputs) + [ANY] * len(after),
         out_specs=[VMEM] * count,
         scratch_shapes=[pltpu.VMEM((fields, lev, tile), F32)] * 3,
         compiler_params=PARAMS,
-        cost_estimate=COST,
+        cost_estimate=COLUMN_COST,
         name=name,
     )(me, *inputs, *after)
 
 
-def edge_kernel(order, count, rows, me_ref, diff_ref, *refs):
-    pieces, low, high = refs[:count], refs[count], refs[count + 1]
+def edge_kernel(order, rows, pieces, me_ref, diff_ref, *refs):
+    count, (low, high) = len(order), refs[-2:]
+    pieces = views(refs, pieces)
     me = me_ref[0]
     for k in range(count):
         row = pick(order, me ^ k)
@@ -323,17 +362,17 @@
 
 
 def edges(me, diff, pieces, order):
-    rows, levels, width = diff.shape
-    shape = pieces[0].shape
-    return pl.pallas_call(
-        functools.partial(edge_kernel, order, len(pieces), rows),
+    rows = diff.shape[0]
+    shape = pieces[0][0].shape
+    return pl.pallas_call(
+        functools.partial(edge_kernel, order, rows, [(None, at) for _, at in pieces]),
         out_shape=[pltpu.VMEM(shape, BF16)] * 2,
         in_specs=[SMEM] + [VMEM] * (1 + len(pieces)),
         out_specs=[VMEM] * 2,
         compiler_params=PARAMS,
         cost_estimate=COST,
         name="edges",
-    )(me, diff, *pieces)
+    )(me, diff, *[array for array, _ in pieces])
 
 
 def final_kernel(table, count, rows, top, me_ref, diff_ref, low_ref, high_ref, pieces, out, held):
@@ -373,7 +412,7 @@
 
     def kernel(*refs):
         final_kernel(
-            table[: len(pieces)], count, rows, top, *refs[:4], refs[4 : 4 + len(needed)], *refs[-2:]
+            table[: len(pieces)], count, rows, top, *refs[:4], views(refs[4:], needed), *refs[-2:]
         )
 
     return pl.pallas_call(
@@ -387,7 +426,7 @@
         compiler_params=PARAMS,
         cost_estimate=COST,
         name=f"final_{top}",
-    )(me, diff, low, high, *needed, *aliased)
+    )(me, diff, low, high, *[array for array, _ in needed], *aliased)
 
 
 def swap(x, distance, count):
@@ -411,29 +450,55 @@
     me = lax.axis_index("lev").astype(jnp.int32).reshape(1)
     split = split_cot(me, cotangent, table, count)
     far_cot = [swap(x, k, count) for k, x in enumerate(split, 1)]
-    edge = edge_rows(state, split[0])
-    low, high = halo(*edge)
-    v_t, w_in_t, w_out_t = transposes(vertical_inverse, w_in, w_out, edge[0])
+    sides = edge_rows(state, split[0])
+    low, high = halo(*sides)
+    v_t, w_in_t, w_out_t = transposes(vertical_inverse, w_in, w_out, sides[0])
     weights = (vertical_inverse, v_t, w_in, w_in_t, w_out_t)
-    after = [far_cot[0], w_in_t]
-    own, diff, far = forward(me, cotangent, state, diffusion, low, high, after, table, count)
-    returned, last = [], []
-
-    def send(pieces):
-        return [swap(x, k, count) for k, x in enumerate(pieces, 1)]
-
-    moved = [send(pieces) for pieces in far[:2]]
+    own_cot, diff, edge, diffused = forward(me, cotangent, state, diffusion, w_in_t, table, count)
+    after = far_cot[:2]
+    firsts = add_halo(me, edge, diff, low, high, sum((x[1:] for x in diffused[:1]), []), after, table[0])
+    owns = [firsts[0]] + [x[0] for x in diffused]
+
+    def send(pieces, first):
+        return [swap(x, k, count) for k, x in enumerate(pieces, first)]
+
+    firsts = send(firsts[1:], 1)
+    arrived = [[(x, c) for x in firsts] for c in range(min(chunks, 2))]
+    returned, last, near, pairs = [], [], [], []
+    behind = [firsts[1], *far_cot[2:]]
     for c in range(chunks):
         if c + 2 < chunks:
-            ready = release(far[c + 2], moved[c] + last)
-            moved.append(send(ready))
-            last = [ready[0]]
-        out = columns(me, own, far_cot, moved[c], c, *weights, last, f"columns_{c}")
+            stack = [x[1] for x in diffused[c + 1 : c + 3]] if c % 2 == 0 else []
+            ready = release(stack, diffused[c + 1][2:], behind + last)
+            if stack:
+                nears = swap(ready[0], 1, count)
+            pieces = send(ready[bool(stack) :], 2)
+            arrived.append([(nears, c % 2)] + [(x, None) for x in pieces])
+            last = [ready[-1]]
+            behind = [nears, pieces[0]]
+        order = last
+        if c == 2:
+            pieces = returned[0][1:]
+            order = last + pieces
+        if c >= 3:
+            if c == 3:
+                pieces = [(x, None) for x in returned[0]]
+                pieces.insert(1, pairs[0])
+                low, high = halo(*edges(me, diff, pieces, table[0]))
+            order = last + returned[c - 2][1:] + [low, high]
+        out = columns(me, own_cot, far_cot, [(owns[c], None)] + arrived[c], c, *weights, near, order, f"columns_{c}")
         last = [out[0]]
-        returned.append([out[0]] + send(out[1:]))
+        near = []
+        if not near:
+            moved_near = swap(out[1], 1, count)
+            pairs += [(moved_near, i) for i in range(out[1].shape[0])]
+        returned.append([out[0]] + send(out[2:], 2))
+    for c, pieces in enumerate(returned):
+        returned[c] = [(x, None) for x in pieces]
+        returned[c].insert(1, pairs[c])
     chunk_of = {row: c for c, order in enumerate(table) for row in order}
-    edge = chunk_of[0]
-    low, high = halo(*edges(me, diff, returned[edge], table[edge]))
+    if chunks < 4:
+        low, high = halo(*edges(me, diff, returned[0], table[0]))
     span = rows // 2
     needed = 1 + max(chunk_of[row] for row in range(span + 1))
     result = final(me, diff, low, high, returned[:needed], table, 0, None)

time: 98.4 us -> 88.6 us (0.900)
  starting transfers between devices: 37.7 us -> 31.5 us
  waiting for transfers between devices: 17.2 us -> 13.5 us
    ppermute x27 -> x23, starting transfers between devices: 25.2 us -> 19 us  [swap(): return lax.ppermute(x, 'lev', [(i, i ^ distance) for i in range(count)])]
    ppermute x2, waiting for transfers between devices: 3.04 us -> 0.01 us  [halo(): lax.ppermute(first, 'hor', backward)]
    ppermute x2, waiting for transfers between devices: 1.13 us -> 0.01 us  [halo(): lax.ppermute(last, 'hor', forward)]
    ppermute x27 -> x23, waiting for transfers between devices: 13.1 us -> 13.5 us  [swap(): return lax.ppermute(x, 'lev', [(i, i ^ distance) for i in range(count)])]
    pallas_call x7 -> x8, Pallas kernels: 20.1 us -> 20.3 us  [the longest x4 20 us: columns(): pl.pallas_call(functools.partial(column_kernel, count, at, tile, paired,...]
  transfers between devices with their start and end apart: 31 -> 27, of which waited for: 9 -> 4; matrix products, arithmetic and copies ran while one was open for 0% -> 0% of each run, Pallas kernels for 37% -> 41%
where the time goes in v1:
time: 88.6 us; the launch traced here: 88.3 us
  Pallas kernels  43.1 us (49%)
  starting transfers between devices  31.5 us (36%)
  waiting for transfers between devices  13.5 us (15%)
    pallas_call x4, Pallas kernels, columns(): pl.pallas_call(functools.partial(column_kernel, count, at, tile, paired,...  20 us
    ppermute x23, starting transfers between devices, swap(): return lax.ppermute(x, 'lev', [(i, i ^ distance) for i in range(count)])  19 us
    ppermute x23, waiting for transfers between devices, swap(): return lax.ppermute(x, 'lev', [(i, i ^ distance) for i in range(count)])  13.5 us
    pallas_call x1, Pallas kernels, forward(): pl.pallas_call(functools.partial(forward_kernel, table, count, rows), out...  8.41 us
    pallas_call x2, Pallas kernels, final(): pl.pallas_call(kernel, out_shape=pltpu.HBM((fields, levels, rows, width),...  7.34 us
    ppermute x2, starting transfers between devices, halo(): lax.ppermute(first, 'hor', backward)  6.77 us
    ppermute x2, starting transfers between devices, halo(): lax.ppermute(last, 'hor', forward)  5.77 us
    pallas_call x1, Pallas kernels, split_cot(): pl.pallas_call(functools.partial(split_kernel, table, count, rows), out_s...  3.41 us
  transfers between devices with their start and end apart: 27, of which 4 were waited for; matrix products, arithmetic and copies ran while one was open for 0% of the time, Pallas kernels for 41%

profile of v1, /device:TPU:25, one launch (start us, length us, event | category | flops | bytes accessed | tf_op | source)
XLA Modules:
  0.0 88.3 jit_solution(4886381024401298823)
XLA Ops:
  0.0 3.4 %split_cot.1 = (bf16[4,2,32,1024]{3,2,1,0:T(8,128)(2,1)S(1)}, bf16[4,2,32,1024]{3,2,1,0:T(8,128)(2,1)S(1)}, bf16[4,2,32,1024]{3,2,1,0:T(8,128)(2,1)S(1)}) custom-call(s32[1]{0:T(128)} %bitcast.me_ref.refs_0_, bf16[2,512,1024]{2,1,0:T(8,128)(2,1)} %bitcast.6), custom_call_target="tpu_custom_call" | custom-call | flops 1 | bytes 1 | tf_op jit(solution)/shard_map/split_cot/pallas_call | solution.py:133
  3.4 1.3 %collective-permute-start.1 = (bf16[4,2,32,1024]{3,2,1,0:T(8,128)(2,1)S(1)}, bf16[4,2,32,1024]{3,2,1,0:T(8,128)(2,1)S(1)}, u32[]{:S(2)}, u32[]{:S(2)}) collective-permute-start(bf16[4,2,32,1024]{3,2,1,0:T(8,128)(2,1)S(1)} %get-tuple-element.60), channel_id=1, source_target_pairs={{0,16},{8,24},{16,0},{24,8},{1,17},{9,25},{17,1},{25,9},{2,18},{10... | collective-permute-start | bytes 1572872 | tf_op jit(solution)/shard_map/ppermute | solution.py:435
  4.7 1.0 %collective-permute-start = (bf16[4,2,32,1024]{3,2,1,0:T(8,128)(2,1)S(1)}, bf16[4,2,32,1024]{3,2,1,0:T(8,128)(2,1)S(1)}, u32[]{:S(2)}, u32[]{:S(2)}) collective-permute-start(bf16[4,2,32,1024]{3,2,1,0:T(8,128)(2,1)S(1)} %get-tuple-element.55.after_ref), channel_id=1, source_target_pairs={{0,8},{8,0},{16,24},{24,16},{1,9},{9,1},{17,25},{25,17},{2,10},{10... | collective-permute-start | bytes 1572872 | tf_op jit(solution)/shard_map/ppermute | solution.py:435
  5.7 3.2 %edge_rows.1 = (bf16[2,32,1024]{2,1,0:T(8,128)(2,1)S(1)}, bf16[2,32,1024]{2,1,0:T(8,128)(2,1)S(1)}) custom-call(f32[2,512,1024]{2,1,0:T(8,128)} %bitcast.4, bf16[4,2,32,1024]{3,2,1,0:T(8,128)(2,1)S(1)} %get-tuple-element.55.after_ref), custom_call_target="tpu_custom_call" | custom-call | flops 1 | bytes 1 | tf_op jit(solution)/shard_map/edge_rows/pallas_call | solution.py:104
  8.9 3.1 %collective-permute-start.3 = (bf16[2,32,1024]{2,1,0:T(8,128)(2,1)S(1)}, bf16[2,32,1024]{2,1,0:T(8,128)(2,1)S(1)}, u32[]{:S(2)}, u32[]{:S(2)}) collective-permute-start(bf16[2,32,1024]{2,1,0:T(8,128)(2,1)S(1)} %get-tuple-element.63), channel_id=1, source_target_pairs={{0,1},{1,2},{2,3},{3,4},{4,5},{5,6},{6,7},{8,9},{9,10},{10,11},{11... | collective-permute-start | bytes 393224 | tf_op jit(solution)/shard_map/ppermute | solution.py:442
  12.1 3.0 %collective-permute-start.4 = (bf16[2,32,1024]{2,1,0:T(8,128)(2,1)S(1)}, bf16[2,32,1024]{2,1,0:T(8,128)(2,1)S(1)}, u32[]{:S(2)}, u32[]{:S(2)}) collective-permute-start(bf16[2,32,1024]{2,1,0:T(8,128)(2,1)S(1)} %get-tuple-element.56.after_ref), channel_id=1, source_target_pairs={{1,0},{2,1},{3,2},{4,3},{5,4},{6,5},{7,6},{9,8},{10,9},{11,10},{12... | collective-permute-start | bytes 393224 | tf_op jit(solution)/shard_map/ppermute | solution.py:442
  15.1 0.8 collective-permute-start.2
  16.3 8.4 %forward.1 = (f32[4,2,32,1024]{3,2,1,0:T(8,128)S(1)}, f32[16,32,1024]{2,1,0:T(8,128)S(1)}, f32[4,2,32,1024]{3,2,1,0:T(8,128)S(1)}, f32[2,32,1024]{2,1,0:T(8,128)...) custom-call(s32[1]{0:T(128)} %bitcast.me_ref.refs_0_, ...), custom_call_target="tpu_custom_call" | custom-call | flops 1 | bytes 1 | tf_op jit(solution)/shard_map/forward/pallas_call | solution.py:228
  25.0 1.3 %collective-permute-start.6 = (bf16[2,2,32,1024]{3,2,1,0:T(8,128)(2,1)S(1)}, bf16[2,2,32,1024]{3,2,1,0:T(8,128)(2,1)S(1)}, u32[]{:S(2)}, u32[]{:S(2)}) collective-permute-start(bf16[2,2,32,1024]{3,2,1,0:T(8,128)(2,1)S(1)} %get-tuple-element.69), channel_id=1, source_target_pairs={{0,16},{8,24},{16,0},{24,8},{1,17},{9,25},{17,1},{25,9},{2,18},{10... | collective-permute-start | bytes 786440 | tf_op jit(solution)/shard_map/ppermute | solution.py:435
  26.3 0.8 collective-permute-start.7
  27.1 2.3 %collective-permute-done.2.refs_5_.refs_2_ = bf16[4,2,32,1024]{3,2,1,0:T(8,128)(2,1)S(1)} collective-permute-done((bf16[4,2,32,1024]{3,2,1,0:T(8,128)(2,1)S(1)}, bf16[4,2,32,1024]{3,2,1,0:T(8,128)(2,1)S(1)}, u32[]{:S(2)}, u32[]{:S(2)}) %collective-permute-start.2) | collective-permute-done | bytes 524320 | tf_op jit(solution)/shard_map/ppermute | solution.py:435
  29.4 5.6 %collective-permute-done.6.refs_4_.refs_5_ = bf16[2,2,32,1024]{3,2,1,0:T(8,128)(2,1)S(1)} collective-permute-done((bf16[2,2,32,1024]{3,2,1,0:T(8,128)(2,1)S(1)}, bf16[2,2,32,1024]{3,2,1,0:T(8,128)(2,1)S(1)}, u32[]{:S(2)}, u32[]{:S(2)}) %collective-permute-start.6) | collective-permute-done | bytes 262176 | tf_op jit(solution)/shard_map/ppermute | solution.py:435
  35.1 0.4 collective-permute-start.14
  35.5 1.9 %collective-permute-start.18 = (bf16[2,32,1024]{2,1,0:T(8,128)(2,1)S(1)}, bf16[2,32,1024]{2,1,0:T(8,128)(2,1)S(1)}, u32[]{:S(2)}, u32[]{:S(2)}) collective-permute-start(bf16[2,32,1024]{2,1,0:T(8,128)(2,1)S(1)} %get-tuple-element.77.refs_12_), channel_id=1, source_target_pairs={{0,24},{8,16},{16,8},{24,0},{1,25},{9,17},{17,9},{25,1},{2,26},{10... | collective-permute-start | bytes 393224 | tf_op jit(solution)/shard_map/ppermute | solution.py:435
  37.5 3.2 %collective-permute-done.7.refs_6_ = bf16[2,2,32,1024]{3,2,1,0:T(8,128)(2,1)S(1)} collective-permute-done((bf16[2,2,32,1024]{3,2,1,0:T(8,128)(2,1)S(1)}, bf16[2,2,32,1024]{3,2,1,0:T(8,128)(2,1)S(1)}, u32[]{:S(2)}, u32[]{:S(2)}) %collective-permute-start.7) | collective-permute-done | bytes 262176 | tf_op jit(solution)/shard_map/ppermute | solution.py:435
  40.7 5.0 %columns_0.1 = (f32[2,32,1024]{2,1,0:T(8,128)S(1)}, f32[1,2,32,1024]{3,2,1,0:T(8,128)S(1)}, bf16[2,32,1024]{2,1,0:T(8,128)(2,1)S(1)}, bf16[2,32,1024]{2,1,0:T(8,128)(2,1)S(1)}) custom-call(s32[1]{0:T(128)} %bitcast.me_ref.refs_0_, f32[4,2,32,1024]{3,2,1,0:T(8,128)S(1)} %get-tuple-element.59.own_cot, ...), custom_call_target="tpu_custom_call" | custom-call | flops 6000000000 | bytes 3000000 | tf_op jit(solution)/shard_map/columns_0/pallas_call | solution.py:333
  46.1 1.7 %collective-permute-start.10 = (bf16[2,32,1024]{2,1,0:T(8,128)(2,1)S(1)}, bf16[2,32,1024]{2,1,0:T(8,128)(2,1)S(1)}, u32[]{:S(2)}, u32[]{:S(2)}) collective-permute-start(bf16[2,32,1024]{2,1,0:T(8,128)(2,1)S(1)} %get-tuple-element.81), channel_id=1, source_target_pairs={{0,24},{8,16},{16,8},{24,0},{1,25},{9,17},{17,9},{25,1},{2,26},{10... | collective-permute-start | bytes 393224 | tf_op jit(solution)/shard_map/ppermute | solution.py:435
  47.8 5.0 %columns_1.1 = (f32[2,32,1024]{2,1,0:T(8,128)S(1)}, f32[1,2,32,1024]{3,2,1,0:T(8,128)S(1)}, bf16[2,32,1024]{2,1,0:T(8,128)(2,1)S(1)}, bf16[2,32,1024]{2,1,0:T(8,128)(2,1)S(1)}) custom-call(s32[1]{0:T(128)} %bitcast.me_ref.refs_0_, f32[4,2,32,1024]{3,2,1,0:T(8,128)S(1)} %get-tuple-element.59.own_cot, ...), custom_call_target="tpu_custom_call" | custom-call | flops 6000000000 | bytes 3000000 | tf_op jit(solution)/shard_map/columns_1/pallas_call | solution.py:333
  52.8 0.4 collective-permute-start.16
  53.2 1.8 %collective-permute-start.23 = (bf16[2,32,1024]{2,1,0:T(8,128)(2,1)S(1)}, bf16[2,32,1024]{2,1,0:T(8,128)(2,1)S(1)}, u32[]{:S(2)}, u32[]{:S(2)}) collective-permute-start(bf16[2,32,1024]{2,1,0:T(8,128)(2,1)S(1)} %get-tuple-element.89.refs_12_), channel_id=1, source_target_pairs={{0,24},{8,16},{16,8},{24,0},{1,25},{9,17},{17,9},{25,1},{2,26},{10... | collective-permute-start | bytes 393224 | tf_op jit(solution)/shard_map/ppermute | solution.py:435
  55.1 1.0 %collective-permute-start.22 = (bf16[2,32,1024]{2,1,0:T(8,128)(2,1)S(1)}, bf16[2,32,1024]{2,1,0:T(8,128)(2,1)S(1)}, u32[]{:S(2)}, u32[]{:S(2)}) collective-permute-start(bf16[2,32,1024]{2,1,0:T(8,128)(2,1)S(1)} %get-tuple-element.100), channel_id=1, source_target_pairs={{0,16},{8,24},{16,0},{24,8},{1,17},{9,25},{17,1},{25,9},{2,18},{10... | collective-permute-start | bytes 393224 | tf_op jit(solution)/shard_map/ppermute | solution.py:435
  56.2 2.6 %collective-permute-start.11 = (bf16[2,32,1024]{2,1,0:T(8,128)(2,1)S(1)}, bf16[2,32,1024]{2,1,0:T(8,128)(2,1)S(1)}, u32[]{:S(2)}, u32[]{:S(2)}) collective-permute-start(bf16[2,32,1024]{2,1,0:T(8,128)(2,1)S(1)} %get-tuple-element.82), channel_id=1, source_target_pairs={{0,1},{1,2},{2,3},{3,4},{4,5},{5,6},{6,7},{8,9},{9,10},{10,11},{11... | collective-permute-start | bytes 393224 | tf_op jit(solution)/shard_map/ppermute | solution.py:442
  58.8 3.7 %collective-permute-start.12 = (bf16[2,32,1024]{2,1,0:T(8,128)(2,1)S(1)}, bf16[2,32,1024]{2,1,0:T(8,128)(2,1)S(1)}, u32[]{:S(2)}, u32[]{:S(2)}) collective-permute-start(bf16[2,32,1024]{2,1,0:T(8,128)(2,1)S(1)} %get-tuple-element.83), channel_id=1, source_target_pairs={{1,0},{2,1},{3,2},{4,3},{5,4},{6,5},{7,6},{9,8},{10,9},{11,10},{12... | collective-permute-start | bytes 393224 | tf_op jit(solution)/shard_map/ppermute | solution.py:442
  62.6 5.0 %columns_2.1 = (f32[2,32,1024]{2,1,0:T(8,128)S(1)}, f32[1,2,32,1024]{3,2,1,0:T(8,128)S(1)}, bf16[2,32,1024]{2,1,0:T(8,128)(2,1)S(1)}, bf16[2,32,1024]{2,1,0:T(8,128)(2,1)S(1)}) custom-call(s32[1]{0:T(128)} %bitcast.me_ref.refs_0_, f32[4,2,32,1024]{3,2,1,0:T(8,128)S(1)} %get-tuple-element.59.own_cot, ...), custom_call_target="tpu_custom_call" | custom-call | flops 6000000000 | bytes 3000000 | tf_op jit(solution)/shard_map/columns_2/pallas_call | solution.py:333
  67.6 0.5 collective-permute-start.20
  68.1 2.8 %collective-permute-start.21 = (bf16[2,32,1024]{2,1,0:T(8,128)(2,1)S(1)}, bf16[2,32,1024]{2,1,0:T(8,128)(2,1)S(1)}, u32[]{:S(2)}, u32[]{:S(2)}) collective-permute-start(bf16[2,32,1024]{2,1,0:T(8,128)(2,1)S(1)} %get-tuple-element.98), channel_id=1, source_target_pairs={{0,24},{8,16},{16,8},{24,0},{1,25},{9,17},{17,9},{25,1},{2,26},{10... | collective-permute-start | bytes 393224 | tf_op jit(solution)/shard_map/ppermute | solution.py:435
  70.9 0.5 collective-permute-start.15
  71.4 5.0 %columns_3.1 = (f32[2,32,1024]{2,1,0:T(8,128)S(1)}, f32[1,2,32,1024]{3,2,1,0:T(8,128)S(1)}, bf16[2,32,1024]{2,1,0:T(8,128)(2,1)S(1)}, bf16[2,32,1024]{2,1,0:T(8,128)(2,1)S(1)}) custom-call(s32[1]{0:T(128)} %bitcast.me_ref.refs_0_, f32[4,2,32,1024]{3,2,1,0:T(8,128)S(1)} %get-tuple-element.59.own_cot, ...), custom_call_target="tpu_custom_call" | custom-call | flops 6000000000 | bytes 3000000 | tf_op jit(solution)/shard_map/columns_3/pallas_call | solution.py:333
  76.9 1.7 %collective-permute-start.26 = (bf16[2,32,1024]{2,1,0:T(8,128)(2,1)S(1)}, bf16[2,32,1024]{2,1,0:T(8,128)(2,1)S(1)}, u32[]{:S(2)}, u32[]{:S(2)}) collective-permute-start(bf16[2,32,1024]{2,1,0:T(8,128)(2,1)S(1)} %get-tuple-element.104), channel_id=1, source_target_pairs={{0,24},{8,16},{16,8},{24,0},{1,25},{9,17},{17,9},{25,1},{2,26},{10... | collective-permute-start | bytes 393224 | tf_op jit(solution)/shard_map/ppermute | solution.py:435
  78.6 3.7 %final_0.1.refs_20_ = f32[2,32,16,1024]{3,2,1,0:T(8,128)} custom-call(s32[1]{0:T(128)} %bitcast.me_ref.refs_0_, f32[16,32,1024]{2,1,0:T(8,128)S(1)} %get-tuple-element.58.diff_ref.refs_1_, bf16[2,32,1024]{2,1,0:T(8,128)(2,1)S(1)} %collective-permute-done.11.refs_15_.refs_2_, bf16[2,32,1024]{2,1,0:T(8,128)(2,1)S(1)} %collective-permute-done.12.refs_16_.refs_3_, ...), custom_call_target="tpu_custom_call" | custom-call | flops 1 | bytes 1 | tf_op jit(solution)/shard_map/final_0/pallas_call | solution.py:418
  82.3 2.3 %collective-permute-done.26.refs_19_ = bf16[2,32,1024]{2,1,0:T(8,128)(2,1)S(1)} collective-permute-done((bf16[2,32,1024]{2,1,0:T(8,128)(2,1)S(1)}, bf16[2,32,1024]{2,1,0:T(8,128)(2,1)S(1)}, u32[]{:S(2)}, u32[]{:S(2)}) %collective-permute-start.26) | collective-permute-done | bytes 131104 | tf_op jit(solution)/shard_map/ppermute | solution.py:435
  84.6 3.7 %final_1.1 = f32[2,32,16,1024]{3,2,1,0:T(8,128)} custom-call(s32[1]{0:T(128)} %bitcast.me_ref.refs_0_, f32[16,32,1024]{2,1,0:T(8,128)S(1)} %get-tuple-element.58.diff_ref.refs_1_, bf16[2,32,1024]{2,1,0:T(8,128)(2,1)S(1)} %collective-permute-done.11.refs_15_.refs_2_, ...), custom_call_target="tpu_custom_call", output_to_operand_aliasing={{}: (20, {})} | custom-call | flops 1 | bytes 1 | tf_op jit(solution)/shard_map/final_1/pallas_call | solution.py:418
  (42 shorter events, 1.8 us)
Async XLA Ops:
  0.0 15.9 %copy-start.1 = (bf16[1024,256]{1,0:T(8,128)(2,1)S(1)}, bf16[1024,256]{1,0:T(8,128)(2,1)}, u32[]{:S(2)}) copy-start(bf16[1024,256]{1,0:T(8,128)(2,1)} %refs_9_.7) | copy-start | bytes 1572868
  0.0 15.9 %copy-start.2 = (f32[2,128,128]{2,1,0:T(8,128)S(1)}, f32[2,128,128]{2,1,0:T(8,128)}, u32[]{:S(2)}) copy-start(f32[2,128,128]{2,1,0:T(8,128)} %refs_7_.7) | copy-start | bytes 393220
  0.0 15.9 %copy-start = (bf16[256,1024]{1,0:T(8,128)(2,1)S(1)}, bf16[256,1024]{1,0:T(8,128)(2,1)}, u32[]{:S(2)}) copy-start(bf16[256,1024]{1,0:T(8,128)(2,1)} %wout_ref.1) | copy-start | bytes 1572868
  3.4 21.3 %collective-permute-start.1 = (bf16[4,2,32,1024]{3,2,1,0:T(8,128)(2,1)S(1)}, bf16[4,2,32,1024]{3,2,1,0:T(8,128)(2,1)S(1)}, u32[]{:S(2)}, u32[]{:S(2)}) collective-permute-start(bf16[4,2,32,1024]{3,2,1,0:T(8,128)(2,1)S(1)} %get-tuple-element.60), channel_id=1, source_target_pairs={{0,16},{8,24},{16,0},{24,8},{1,17},{9,25},{17,1},{25,9},{2,18},{10... | collective-permute-start | bytes 1572872 | tf_op jit(solution)/shard_map/ppermute | solution.py:435
  4.7 20.0 %collective-permute-start = (bf16[4,2,32,1024]{3,2,1,0:T(8,128)(2,1)S(1)}, bf16[4,2,32,1024]{3,2,1,0:T(8,128)(2,1)S(1)}, u32[]{:S(2)}, u32[]{:S(2)}) collective-permute-start(bf16[4,2,32,1024]{3,2,1,0:T(8,128)(2,1)S(1)} %get-tuple-element.55.after_ref), channel_id=1, source_target_pairs={{0,8},{8,0},{16,24},{24,16},{1,9},{9,1},{17,25},{25,17},{2,10},{10... | collective-permute-start | bytes 1572872 | tf_op jit(solution)/shard_map/ppermute | solution.py:435
  8.9 15.8 %collective-permute-start.3 = (bf16[2,32,1024]{2,1,0:T(8,128)(2,1)S(1)}, bf16[2,32,1024]{2,1,0:T(8,128)(2,1)S(1)}, u32[]{:S(2)}, u32[]{:S(2)}) collective-permute-start(bf16[2,32,1024]{2,1,0:T(8,128)(2,1)S(1)} %get-tuple-element.63), channel_id=1, source_target_pairs={{0,1},{1,2},{2,3},{3,4},{4,5},{5,6},{6,7},{8,9},{9,10},{10,11},{11... | collective-permute-start | bytes 393224 | tf_op jit(solution)/shard_map/ppermute | solution.py:442
  12.1 12.6 %collective-permute-start.4 = (bf16[2,32,1024]{2,1,0:T(8,128)(2,1)S(1)}, bf16[2,32,1024]{2,1,0:T(8,128)(2,1)S(1)}, u32[]{:S(2)}, u32[]{:S(2)}) collective-permute-start(bf16[2,32,1024]{2,1,0:T(8,128)(2,1)S(1)} %get-tuple-element.56.after_ref), channel_id=1, source_target_pairs={{1,0},{2,1},{3,2},{4,3},{5,4},{6,5},{7,6},{9,8},{10,9},{11,10},{12... | collective-permute-start | bytes 393224 | tf_op jit(solution)/shard_map/ppermute | solution.py:442
  15.1 14.3 %collective-permute-start.2 = (bf16[4,2,32,1024]{3,2,1,0:T(8,128)(2,1)S(1)}, bf16[4,2,32,1024]{3,2,1,0:T(8,128)(2,1)S(1)}, u32[]{:S(2)}, u32[]{:S(2)}) collective-permute-start(bf16[4,2,32,1024]{3,2,1,0:T(8,128)(2,1)S(1)} %get-tuple-element.61), channel_id=1, source_target_pairs={{0,24},{8,16},{16,8},{24,0},{1,25},{9,17},{17,9},{25,1},{2,26},{10... | collective-permute-start | bytes 1572872 | tf_op jit(solution)/shard_map/ppermute | solution.py:435
  24.9 15.7 %collective-permute-start.5 = (f32[2,2,32,1024]{3,2,1,0:T(8,128)S(1)}, f32[2,2,32,1024]{3,2,1,0:T(8,128)S(1)}, u32[]{:S(2)}, u32[]{:S(2)}) collective-permute-start(f32[2,2,32,1024]{3,2,1,0:T(8,128)S(1)} %get-tuple-element.68), channel_id=1, source_target_pairs={{0,8},{8,0},{16,24},{24,16},{1,9},{9,1},{17,25},{25,17},{2,10},{10... | collective-permute-start | bytes 1572872 | tf_op jit(solution)/shard_map/ppermute | solution.py:435
  25.0 10.0 %collective-permute-start.6 = (bf16[2,2,32,1024]{3,2,1,0:T(8,128)(2,1)S(1)}, bf16[2,2,32,1024]{3,2,1,0:T(8,128)(2,1)S(1)}, u32[]{:S(2)}, u32[]{:S(2)}) collective-permute-start(bf16[2,2,32,1024]{3,2,1,0:T(8,128)(2,1)S(1)} %get-tuple-element.69), channel_id=1, source_target_pairs={{0,16},{8,24},{16,0},{24,8},{1,17},{9,25},{17,1},{25,9},{2,18},{10... | collective-permute-start | bytes 786440 | tf_op jit(solution)/shard_map/ppermute | solution.py:435
  26.3 14.4 %collective-permute-start.7 = (bf16[2,2,32,1024]{3,2,1,0:T(8,128)(2,1)S(1)}, bf16[2,2,32,1024]{3,2,1,0:T(8,128)(2,1)S(1)}, u32[]{:S(2)}, u32[]{:S(2)}) collective-permute-start(bf16[2,2,32,1024]{3,2,1,0:T(8,128)(2,1)S(1)} %get-tuple-element.70), channel_id=1, source_target_pairs={{0,24},{8,16},{16,8},{24,0},{1,25},{9,17},{17,9},{25,1},{2,26},{10... | collective-permute-start | bytes 786440 | tf_op jit(solution)/shard_map/ppermute | solution.py:435
  35.1 12.6 %collective-permute-start.14 = (bf16[2,32,1024]{2,1,0:T(8,128)(2,1)S(1)}, bf16[2,32,1024]{2,1,0:T(8,128)(2,1)S(1)}, u32[]{:S(2)}, u32[]{:S(2)}) collective-permute-start(bf16[2,32,1024]{2,1,0:T(8,128)(2,1)S(1)} %get-tuple-element.88), channel_id=1, source_target_pairs={{0,16},{8,24},{16,0},{24,8},{1,17},{9,25},{17,1},{25,9},{2,18},{10... | collective-permute-start | bytes 393224 | tf_op jit(solution)/shard_map/ppermute | solution.py:435
  35.5 20.6 %collective-permute-start.18 = (bf16[2,32,1024]{2,1,0:T(8,128)(2,1)S(1)}, bf16[2,32,1024]{2,1,0:T(8,128)(2,1)S(1)}, u32[]{:S(2)}, u32[]{:S(2)}) collective-permute-start(bf16[2,32,1024]{2,1,0:T(8,128)(2,1)S(1)} %get-tuple-element.77.refs_12_), channel_id=1, source_target_pairs={{0,24},{8,16},{16,8},{24,0},{1,25},{9,17},{17,9},{25,1},{2,26},{10... | collective-permute-start | bytes 393224 | tf_op jit(solution)/shard_map/ppermute | solution.py:435
  37.5 10.3 %collective-permute-start.13 = (f32[2,2,32,1024]{3,2,1,0:T(8,128)S(1)}, f32[2,2,32,1024]{3,2,1,0:T(8,128)S(1)}, u32[]{:S(2)}, u32[]{:S(2)}) collective-permute-start(f32[2,2,32,1024]{3,2,1,0:T(8,128)S(1)} %get-tuple-element.87), channel_id=1, source_target_pairs={{0,8},{8,0},{16,24},{24,16},{1,9},{9,1},{17,25},{25,17},{2,10},{10... | collective-permute-start | bytes 1572872 | tf_op jit(solution)/shard_map/ppermute | solution.py:435
  45.6 7.6 %collective-permute-start.9 = (bf16[2,32,1024]{2,1,0:T(8,128)(2,1)S(1)}, bf16[2,32,1024]{2,1,0:T(8,128)(2,1)S(1)}, u32[]{:S(2)}, u32[]{:S(2)}) collective-permute-start(bf16[2,32,1024]{2,1,0:T(8,128)(2,1)S(1)} %get-tuple-element.80), channel_id=1, source_target_pairs={{0,16},{8,24},{16,0},{24,8},{1,17},{9,25},{17,1},{25,9},{2,18},{10... | collective-permute-start | bytes 393224 | tf_op jit(solution)/shard_map/ppermute | solution.py:435
  46.1 8.9 %collective-permute-start.10 = (bf16[2,32,1024]{2,1,0:T(8,128)(2,1)S(1)}, bf16[2,32,1024]{2,1,0:T(8,128)(2,1)S(1)}, u32[]{:S(2)}, u32[]{:S(2)}) collective-permute-start(bf16[2,32,1024]{2,1,0:T(8,128)(2,1)S(1)} %get-tuple-element.81), channel_id=1, source_target_pairs={{0,24},{8,16},{16,8},{24,0},{1,25},{9,17},{17,9},{25,1},{2,26},{10... | collective-permute-start | bytes 393224 | tf_op jit(solution)/shard_map/ppermute | solution.py:435
  47.7 7.3 %collective-permute-start.8 = (f32[1,2,32,1024]{3,2,1,0:T(8,128)S(1)}, f32[1,2,32,1024]{3,2,1,0:T(8,128)S(1)}, u32[]{:S(2)}, u32[]{:S(2)}) collective-permute-start(f32[1,2,32,1024]{3,2,1,0:T(8,128)S(1)} %get-tuple-element.79), channel_id=1, source_target_pairs={{0,8},{8,0},{16,24},{24,16},{1,9},{9,1},{17,25},{25,17},{2,10},{10... | collective-permute-start | bytes 786440 | tf_op jit(solution)/shard_map/ppermute | solution.py:435
  52.8 6.0 %collective-permute-start.16 = (bf16[2,32,1024]{2,1,0:T(8,128)(2,1)S(1)}, bf16[2,32,1024]{2,1,0:T(8,128)(2,1)S(1)}, u32[]{:S(2)}, u32[]{:S(2)}) collective-permute-start(bf16[2,32,1024]{2,1,0:T(8,128)(2,1)S(1)} %get-tuple-element.92), channel_id=1, source_target_pairs={{0,16},{8,24},{16,0},{24,8},{1,17},{9,25},{17,1},{25,9},{2,18},{10... | collective-permute-start | bytes 393224 | tf_op jit(solution)/shard_map/ppermute | solution.py:435
  53.2 17.7 %collective-permute-start.23 = (bf16[2,32,1024]{2,1,0:T(8,128)(2,1)S(1)}, bf16[2,32,1024]{2,1,0:T(8,128)(2,1)S(1)}, u32[]{:S(2)}, u32[]{:S(2)}) collective-permute-start(bf16[2,32,1024]{2,1,0:T(8,128)(2,1)S(1)} %get-tuple-element.89.refs_12_), channel_id=1, source_target_pairs={{0,24},{8,16},{16,8},{24,0},{1,25},{9,17},{17,9},{25,1},{2,26},{10... | collective-permute-start | bytes 393224 | tf_op jit(solution)/shard_map/ppermute | solution.py:435
  55.0 12.6 %collective-permute-start.17 = (bf16[2,32,1024]{2,1,0:T(8,128)(2,1)S(1)}, bf16[2,32,1024]{2,1,0:T(8,128)(2,1)S(1)}, u32[]{:S(2)}, u32[]{:S(2)}) collective-permute-start(bf16[2,32,1024]{2,1,0:T(8,128)(2,1)S(1)} %get-tuple-element.93), channel_id=1, source_target_pairs={{0,24},{8,16},{16,8},{24,0},{1,25},{9,17},{17,9},{25,1},{2,26},{10... | collective-permute-start | bytes 393224 | tf_op jit(solution)/shard_map/ppermute | solution.py:435
  55.1 13.0 %collective-permute-start.22 = (bf16[2,32,1024]{2,1,0:T(8,128)(2,1)S(1)}, bf16[2,32,1024]{2,1,0:T(8,128)(2,1)S(1)}, u32[]{:S(2)}, u32[]{:S(2)}) collective-permute-start(bf16[2,32,1024]{2,1,0:T(8,128)(2,1)S(1)} %get-tuple-element.100), channel_id=1, source_target_pairs={{0,16},{8,24},{16,0},{24,8},{1,17},{9,25},{17,1},{25,9},{2,18},{10... | collective-permute-start | bytes 393224 | tf_op jit(solution)/shard_map/ppermute | solution.py:435
  56.2 14.8 %collective-permute-start.11 = (bf16[2,32,1024]{2,1,0:T(8,128)(2,1)S(1)}, bf16[2,32,1024]{2,1,0:T(8,128)(2,1)S(1)}, u32[]{:S(2)}, u32[]{:S(2)}) collective-permute-start(bf16[2,32,1024]{2,1,0:T(8,128)(2,1)S(1)} %get-tuple-element.82), channel_id=1, source_target_pairs={{0,1},{1,2},{2,3},{3,4},{4,5},{5,6},{6,7},{8,9},{9,10},{10,11},{11... | collective-permute-start | bytes 393224 | tf_op jit(solution)/shard_map/ppermute | solution.py:442
  58.8 12.6 %collective-permute-start.12 = (bf16[2,32,1024]{2,1,0:T(8,128)(2,1)S(1)}, bf16[2,32,1024]{2,1,0:T(8,128)(2,1)S(1)}, u32[]{:S(2)}, u32[]{:S(2)}) collective-permute-start(bf16[2,32,1024]{2,1,0:T(8,128)(2,1)S(1)} %get-tuple-element.83), channel_id=1, source_target_pairs={{1,0},{2,1},{3,2},{4,3},{5,4},{6,5},{7,6},{9,8},{10,9},{11,10},{12... | collective-permute-start | bytes 393224 | tf_op jit(solution)/shard_map/ppermute | solution.py:442
  67.6 9.0 %collective-permute-start.20 = (bf16[2,32,1024]{2,1,0:T(8,128)(2,1)S(1)}, bf16[2,32,1024]{2,1,0:T(8,128)(2,1)S(1)}, u32[]{:S(2)}, u32[]{:S(2)}) collective-permute-start(bf16[2,32,1024]{2,1,0:T(8,128)(2,1)S(1)} %get-tuple-element.97), channel_id=1, source_target_pairs={{0,16},{8,24},{16,0},{24,8},{1,17},{9,25},{17,1},{25,9},{2,18},{10... | collective-permute-start | bytes 393224 | tf_op jit(solution)/shard_map/ppermute | solution.py:435
  68.1 8.8 %collective-permute-start.21 = (bf16[2,32,1024]{2,1,0:T(8,128)(2,1)S(1)}, bf16[2,32,1024]{2,1,0:T(8,128)(2,1)S(1)}, u32[]{:S(2)}, u32[]{:S(2)}) collective-permute-start(bf16[2,32,1024]{2,1,0:T(8,128)(2,1)S(1)} %get-tuple-element.98), channel_id=1, source_target_pairs={{0,24},{8,16},{16,8},{24,0},{1,25},{9,17},{17,9},{25,1},{2,26},{10... | collective-permute-start | bytes 393224 | tf_op jit(solution)/shard_map/ppermute | solution.py:435
  70.9 7.7 %collective-permute-start.19 = (f32[1,2,32,1024]{3,2,1,0:T(8,128)S(1)}, f32[1,2,32,1024]{3,2,1,0:T(8,128)S(1)}, u32[]{:S(2)}, u32[]{:S(2)}) collective-permute-start(f32[1,2,32,1024]{3,2,1,0:T(8,128)S(1)} %get-tuple-element.96), channel_id=1, source_target_pairs={{0,8},{8,0},{16,24},{24,16},{1,9},{9,1},{17,25},{25,17},{2,10},{10... | collective-permute-start | bytes 786440 | tf_op jit(solution)/shard_map/ppermute | solution.py:435
  70.9 7.7 %collective-permute-start.15 = (f32[1,2,32,1024]{3,2,1,0:T(8,128)S(1)}, f32[1,2,32,1024]{3,2,1,0:T(8,128)S(1)}, u32[]{:S(2)}, u32[]{:S(2)}) collective-permute-start(f32[1,2,32,1024]{3,2,1,0:T(8,128)S(1)} %get-tuple-element.91), channel_id=1, source_target_pairs={{0,8},{8,0},{16,24},{24,16},{1,9},{9,1},{17,25},{25,17},{2,10},{10... | collective-permute-start | bytes 786440 | tf_op jit(solution)/shard_map/ppermute | solution.py:435
  76.4 8.2 %collective-permute-start.24 = (f32[1,2,32,1024]{3,2,1,0:T(8,128)S(1)}, f32[1,2,32,1024]{3,2,1,0:T(8,128)S(1)}, u32[]{:S(2)}, u32[]{:S(2)}) collective-permute-start(f32[1,2,32,1024]{3,2,1,0:T(8,128)S(1)} %get-tuple-element.102), channel_id=1, source_target_pairs={{0,8},{8,0},{16,24},{24,16},{1,9},{9,1},{17,25},{25,17},{2,10},{10... | collective-permute-start | bytes 786440 | tf_op jit(solution)/shard_map/ppermute | solution.py:435
  76.6 5.8 %collective-permute-start.25 = (bf16[2,32,1024]{2,1,0:T(8,128)(2,1)S(1)}, bf16[2,32,1024]{2,1,0:T(8,128)(2,1)S(1)}, u32[]{:S(2)}, u32[]{:S(2)}) collective-permute-start(bf16[2,32,1024]{2,1,0:T(8,128)(2,1)S(1)} %get-tuple-element.103), channel_id=1, source_target_pairs={{0,16},{8,24},{16,0},{24,8},{1,17},{9,25},{17,1},{25,9},{2,18},{10... | collective-permute-start | bytes 393224 | tf_op jit(solution)/shard_map/ppermute | solution.py:435
  76.9 7.7 %collective-permute-start.26 = (bf16[2,32,1024]{2,1,0:T(8,128)(2,1)S(1)}, bf16[2,32,1024]{2,1,0:T(8,128)(2,1)S(1)}, u32[]{:S(2)}, u32[]{:S(2)}) collective-permute-start(bf16[2,32,1024]{2,1,0:T(8,128)(2,1)S(1)} %get-tuple-element.104), channel_id=1, source_target_pairs={{0,24},{8,16},{16,8},{24,0},{1,25},{9,17},{17,9},{25,1},{2,26},{10... | collective-permute-start | bytes 393224 | tf_op jit(solution)/shard_map/ppermute | solution.py:435

commit v2 on v1

--- a/solution.py
+++ b/solution.py
@@ -11,8 +11,8 @@
 VMEM_MIB = 20
 PARAMS = pltpu.CompilerParams(vmem_limit_bytes=VMEM_MIB * 1024 * 1024)
 COST = pl.CostEstimate(flops=1, bytes_accessed=1, transcendentals=0)
-COLUMN_COST = pl.CostEstimate(flops=6_000_000_000, bytes_accessed=1, transcendentals=0)
-COLUMN_COST = pl.CostEstimate(flops=6_000_000_000, bytes_accessed=3_000_000, transcendentals=0)
+COLUMN_COST = pl.CostEstimate(flops=4_000_000_000, bytes_accessed=1, transcendentals=0)
+COLUMN_COST = pl.CostEstimate(flops=4_000_000_000, bytes_accessed=3_000_000, transcendentals=0)
 VMEM = pl.BlockSpec(memory_space=pltpu.VMEM)
 ANY = pl.BlockSpec(memory_space=pl.ANY)
 SMEM = pl.BlockSpec(memory_space=pltpu.SMEM)
@@ -280,7 +280,7 @@
     return dot(m_top, x_top) + (dot(m_rest, x_top) + dot(m_top, x_rest))
 
 
-def column_kernel(count, at, tile, paired, places, me_ref, own_cot, *refs):
+def column_kernel(count, at, tile, places, me_ref, own_cot, *refs):
     far_cot, states = refs[: count - 1], views(refs[count - 1 : 2 * count - 1], places)
     v_ref, vt_ref, win_ref, wint_ref, woutt_ref = refs[2 * count - 1 : 2 * count + 4]
     outs, (cols, cot_cols, back) = refs[-count - 3 : -3], refs[-3:]
@@ -299,7 +299,7 @@
     )
     cot = jnp.concatenate([cot_cols[f] for f in range(fields)], axis=0)
     cot_half = cot.astype(BF16)
-    hidden, block = win_ref.shape[0], 256
+    hidden, block = win_ref.shape[0], 512
     grad = cot
     for h in range(0, hidden, block):
         preact = dot(win_ref[h : h + block, :], inputs)
@@ -312,27 +312,18 @@
     for k in range(count):
         to = pl.ds(pl.multiple_of((me ^ k) * levels, levels), levels)
         for f in range(fields):
-            value = back[f, to, :].astype(outs[k].dtype)
-            if k == 1:
-                outs[k][len(paired), f, :, lanes] = value
-                for ref in paired:
-                    outs[k][0, f, :, lanes] = refs[ref][0, f, :, lanes]
-            else:
-                outs[k][f, :, lanes] = value
-
-
-def columns(me, own_cot, far_cot, states, at, v, vt, w_in, w_in_t, w_out_t, earlier, after, name):
+            outs[k][f, :, lanes] = back[f, to, :].astype(outs[k].dtype)
+
+
+def columns(me, own_cot, far_cot, states, at, v, vt, w_in, w_in_t, w_out_t, after, name):
     count = len(states)
     fields, levels, width = states[0][0].shape
     lev = v.shape[1]
-    tile = min(width, 512)
-    inputs = (own_cot, *far_cot, *[array for array, _ in states], v, vt, w_in, w_in_t, w_out_t, *earlier)
-    shapes = [(fields, levels, width)] * count
-    shapes[1] = (1 + len(earlier), *shapes[1])
-    paired = [len(inputs) - 2] if earlier else []
-    return pl.pallas_call(
-        functools.partial(column_kernel, count, at, tile, paired, [(None, place) for _, place in states]),
-        out_shape=[pltpu.VMEM(dims, link_type(k)) for k, dims in enumerate(shapes)],
+    tile = min(width, 1024)
+    inputs = (own_cot, *far_cot, *[array for array, _ in states], v, vt, w_in, w_in_t, w_out_t)
+    return pl.pallas_call(
+        functools.partial(column_kernel, count, at, tile, [(None, place) for _, place in states]),
+        out_shape=[pltpu.VMEM((fields, levels, width), link_type(k)) for k in range(count)],
         grid=(width // tile,),
         in_specs=[SMEM] + [VMEM] * len(inputs) + [ANY] * len(after),
         out_specs=[VMEM] * count,
@@ -343,9 +334,9 @@
     )(me, *inputs, *after)
 
 
-def edge_kernel(order, rows, pieces, me_ref, diff_ref, *refs):
+def edge_kernel(order, rows, me_ref, diff_ref, *refs):
     count, (low, high) = len(order), refs[-2:]
-    pieces = views(refs, pieces)
+    pieces = refs[:count]
     me = me_ref[0]
     for k in range(count):
         row = pick(order, me ^ k)
@@ -363,16 +354,16 @@
 
 def edges(me, diff, pieces, order):
     rows = diff.shape[0]
-    shape = pieces[0][0].shape
-    return pl.pallas_call(
-        functools.partial(edge_kernel, order, rows, [(None, at) for _, at in pieces]),
+    shape = pieces[0].shape
+    return pl.pallas_call(
+        functools.partial(edge_kernel, order, rows),
         out_shape=[pltpu.VMEM(shape, BF16)] * 2,
         in_specs=[SMEM] + [VMEM] * (1 + len(pieces)),
         out_specs=[VMEM] * 2,
         compiler_params=PARAMS,
         cost_estimate=COST,
         name="edges",
-    )(me, diff, *[array for array, _ in pieces])
+    )(me, diff, *pieces)
 
 
 def final_kernel(table, count, rows, top, me_ref, diff_ref, low_ref, high_ref, pieces, out, held):
@@ -412,7 +403,7 @@
 
     def kernel(*refs):
         final_kernel(
-            table[: len(pieces)], count, rows, top, *refs[:4], views(refs[4:], needed), *refs[-2:]
+            table[: len(pieces)], count, rows, top, *refs[:4], refs[4 : 4 + len(needed)], *refs[-2:]
         )
 
     return pl.pallas_call(
@@ -426,7 +417,7 @@
         compiler_params=PARAMS,
         cost_estimate=COST,
         name=f"final_{top}",
-    )(me, diff, low, high, *[array for array, _ in needed], *aliased)
+    )(me, diff, low, high, *needed, *aliased)
 
 
 def swap(x, distance, count):
@@ -464,7 +455,7 @@
 
     firsts = send(firsts[1:], 1)
     arrived = [[(x, c) for x in firsts] for c in range(min(chunks, 2))]
-    returned, last, near, pairs = [], [], [], []
+    returned, last = [], []
     behind = [firsts[1], *far_cot[2:]]
     for c in range(chunks):
         if c + 2 < chunks:
@@ -478,24 +469,15 @@
             behind = [nears, pieces[0]]
         order = last
         if c == 2:
-            pieces = returned[0][1:]
-            order = last + pieces
+            order = last + returned[0][2:]
         if c >= 3:
             if c == 3:
-                pieces = [(x, None) for x in returned[0]]
-                pieces.insert(1, pairs[0])
-                low, high = halo(*edges(me, diff, pieces, table[0]))
-            order = last + returned[c - 2][1:] + [low, high]
-        out = columns(me, own_cot, far_cot, [(owns[c], None)] + arrived[c], c, *weights, near, order, f"columns_{c}")
+                low, high = halo(*edges(me, diff, returned[0], table[0]))
+            order = last + returned[c - 2][2:] + [low, high]
+        states = [(owns[c], None)] + arrived[c]
+        out = columns(me, own_cot, far_cot, states, c, *weights, order, f"columns_{c}")
         last = [out[0]]
-        near = []
-        if not near:
-            moved_near = swap(out[1], 1, count)
-            pairs += [(moved_near, i) for i in range(out[1].shape[0])]
-        returned.append([out[0]] + send(out[2:], 2))
-    for c, pieces in enumerate(returned):
-        returned[c] = [(x, None) for x in pieces]
-        returned[c].insert(1, pairs[c])
+        returned.append([out[0]] + send(out[1:], 1))
     chunk_of = {row: c for c, order in enumerate(table) for row in order}
     if chunks < 4:
         low, high = halo(*edges(me, diff, returned[0], table[0]))

time: 88.6 us -> 83.2 us (0.939)
  Pallas kernels: 43.1 us -> 38.3 us
    pallas_call x5, Pallas kernels: 20 us -> 15.2 us  [the longest x4 15.2 us: columns(): pl.pallas_call(functools.partial(column_kernel, count, at, tile, [(None,...]
    ppermute x2, starting transfers between devices: 5.77 us -> 7.15 us  [halo(): lax.ppermute(last, 'hor', forward)]
    ppermute x2, starting transfers between devices: 6.77 us -> 5.39 us  [halo(): lax.ppermute(first, 'hor', backward)]
  transfers between devices with their start and end apart: 27 -> 27, of which waited for: 4 -> 5; matrix products, arithmetic and copies ran while one was open for 0% -> 0% of each run, Pallas kernels for 41% -> 38%
where the time goes in v2:
time: 83.2 us; the launch traced here: 82.9 us
  Pallas kernels  38.3 us (46%)
  starting transfers between devices  31.7 us (38%)
  waiting for transfers between devices  12.7 us (15%)
    ppermute x23, starting transfers between devices, swap(): return lax.ppermute(x, 'lev', [(i, i ^ distance) for i in range(count)])  19.1 us
    pallas_call x4, Pallas kernels, columns(): pl.pallas_call(functools.partial(column_kernel, count, at, tile, [(None,...  15.2 us
    ppermute x23, waiting for transfers between devices, swap(): return lax.ppermute(x, 'lev', [(i, i ^ distance) for i in range(count)])  12.7 us
    pallas_call x1, Pallas kernels, forward(): pl.pallas_call(functools.partial(forward_kernel, table, count, rows), out...  8.43 us
    pallas_call x2, Pallas kernels, final(): pl.pallas_call(kernel, out_shape=pltpu.HBM((fields, levels, rows, width),...  7.34 us
    ppermute x2, starting transfers between devices, halo(): lax.ppermute(last, 'hor', forward)  7.15 us
    ppermute x2, starting transfers between devices, halo(): lax.ppermute(first, 'hor', backward)  5.39 us
    pallas_call x1, Pallas kernels, split_cot(): pl.pallas_call(functools.partial(split_kernel, table, count, rows), out_s...  3.41 us
  transfers between devices with their start and end apart: 27, of which 5 were waited for; matrix products, arithmetic and copies ran while one was open for 0% of the time, Pallas kernels for 38%

profile of v2, /device:TPU:25, one launch (start us, length us, event | category | flops | bytes accessed | tf_op | source)
XLA Modules:
  0.0 82.9 jit_solution(10658724370868831415)
XLA Ops:
  0.0 3.4 %split_cot.1 = (bf16[4,2,32,1024]{3,2,1,0:T(8,128)(2,1)S(1)}, bf16[4,2,32,1024]{3,2,1,0:T(8,128)(2,1)S(1)}, bf16[4,2,32,1024]{3,2,1,0:T(8,128)(2,1)S(1)}) custom-call(s32[1]{0:T(128)} %bitcast.me_ref.refs_0_, bf16[2,512,1024]{2,1,0:T(8,128)(2,1)} %bitcast.6), custom_call_target="tpu_custom_call" | custom-call | flops 1 | bytes 1 | tf_op jit(solution)/shard_map/split_cot/pallas_call | solution.py:133
  3.4 1.3 %collective-permute-start.1 = (bf16[4,2,32,1024]{3,2,1,0:T(8,128)(2,1)S(1)}, bf16[4,2,32,1024]{3,2,1,0:T(8,128)(2,1)S(1)}, u32[]{:S(2)}, u32[]{:S(2)}) collective-permute-start(bf16[4,2,32,1024]{3,2,1,0:T(8,128)(2,1)S(1)} %get-tuple-element.60), channel_id=1, source_target_pairs={{0,16},{8,24},{16,0},{24,8},{1,17},{9,25},{17,1},{25,9},{2,18},{10... | collective-permute-start | bytes 1572872 | tf_op jit(solution)/shard_map/ppermute | solution.py:426
  4.7 1.0 %collective-permute-start = (bf16[4,2,32,1024]{3,2,1,0:T(8,128)(2,1)S(1)}, bf16[4,2,32,1024]{3,2,1,0:T(8,128)(2,1)S(1)}, u32[]{:S(2)}, u32[]{:S(2)}) collective-permute-start(bf16[4,2,32,1024]{3,2,1,0:T(8,128)(2,1)S(1)} %get-tuple-element.55.after_ref), channel_id=1, source_target_pairs={{0,8},{8,0},{16,24},{24,16},{1,9},{9,1},{17,25},{25,17},{2,10},{10... | collective-permute-start | bytes 1572872 | tf_op jit(solution)/shard_map/ppermute | solution.py:426
  5.8 3.2 %edge_rows.1 = (bf16[2,32,1024]{2,1,0:T(8,128)(2,1)S(1)}, bf16[2,32,1024]{2,1,0:T(8,128)(2,1)S(1)}) custom-call(f32[2,512,1024]{2,1,0:T(8,128)} %bitcast.4, bf16[4,2,32,1024]{3,2,1,0:T(8,128)(2,1)S(1)} %get-tuple-element.55.after_ref), custom_call_target="tpu_custom_call" | custom-call | flops 1 | bytes 1 | tf_op jit(solution)/shard_map/edge_rows/pallas_call | solution.py:104
  9.0 3.1 %collective-permute-start.3 = (bf16[2,32,1024]{2,1,0:T(8,128)(2,1)S(1)}, bf16[2,32,1024]{2,1,0:T(8,128)(2,1)S(1)}, u32[]{:S(2)}, u32[]{:S(2)}) collective-permute-start(bf16[2,32,1024]{2,1,0:T(8,128)(2,1)S(1)} %get-tuple-element.63), channel_id=1, source_target_pairs={{0,1},{1,2},{2,3},{3,4},{4,5},{5,6},{6,7},{8,9},{9,10},{10,11},{11... | collective-permute-start | bytes 393224 | tf_op jit(solution)/shard_map/ppermute | solution.py:433
  12.2 3.0 %collective-permute-start.4 = (bf16[2,32,1024]{2,1,0:T(8,128)(2,1)S(1)}, bf16[2,32,1024]{2,1,0:T(8,128)(2,1)S(1)}, u32[]{:S(2)}, u32[]{:S(2)}) collective-permute-start(bf16[2,32,1024]{2,1,0:T(8,128)(2,1)S(1)} %get-tuple-element.56.after_ref), channel_id=1, source_target_pairs={{1,0},{2,1},{3,2},{4,3},{5,4},{6,5},{7,6},{9,8},{10,9},{11,10},{12... | collective-permute-start | bytes 393224 | tf_op jit(solution)/shard_map/ppermute | solution.py:433
  15.7 8.4 %forward.1 = (f32[4,2,32,1024]{3,2,1,0:T(8,128)S(1)}, f32[16,32,1024]{2,1,0:T(8,128)S(1)}, f32[4,2,32,1024]{3,2,1,0:T(8,128)S(1)}, f32[2,32,1024]{2,1,0:T(8,128)...) custom-call(s32[1]{0:T(128)} %bitcast.me_ref.refs_0_, ...), custom_call_target="tpu_custom_call" | custom-call | flops 1 | bytes 1 | tf_op jit(solution)/shard_map/forward/pallas_call | solution.py:228
  24.3 1.1 %collective-permute-start.5 = (f32[2,2,32,1024]{3,2,1,0:T(8,128)S(1)}, f32[2,2,32,1024]{3,2,1,0:T(8,128)S(1)}, u32[]{:S(2)}, u32[]{:S(2)}) collective-permute-start(f32[2,2,32,1024]{3,2,1,0:T(8,128)S(1)} %get-tuple-element.68), channel_id=1, source_target_pairs={{0,8},{8,0},{16,24},{24,16},{1,9},{9,1},{17,25},{25,17},{2,10},{10... | collective-permute-start | bytes 1572872 | tf_op jit(solution)/shard_map/ppermute | solution.py:426
  25.5 1.2 %collective-permute-start.6 = (bf16[2,2,32,1024]{3,2,1,0:T(8,128)(2,1)S(1)}, bf16[2,2,32,1024]{3,2,1,0:T(8,128)(2,1)S(1)}, u32[]{:S(2)}, u32[]{:S(2)}) collective-permute-start(bf16[2,2,32,1024]{3,2,1,0:T(8,128)(2,1)S(1)} %get-tuple-element.69), channel_id=1, source_target_pairs={{0,16},{8,24},{16,0},{24,8},{1,17},{9,25},{17,1},{25,9},{2,18},{10... | collective-permute-start | bytes 786440 | tf_op jit(solution)/shard_map/ppermute | solution.py:426
  27.2 1.6 %collective-permute-done.2.refs_5_.refs_2_ = bf16[4,2,32,1024]{3,2,1,0:T(8,128)(2,1)S(1)} collective-permute-done((bf16[4,2,32,1024]{3,2,1,0:T(8,128)(2,1)S(1)}, bf16[4,2,32,1024]{3,2,1,0:T(8,128)(2,1)S(1)}, u32[]{:S(2)}, u32[]{:S(2)}) %collective-permute-start.2) | collective-permute-done | bytes 524320 | tf_op jit(solution)/shard_map/ppermute | solution.py:426
  28.8 5.1 %collective-permute-done.6.refs_4_.refs_5_ = bf16[2,2,32,1024]{3,2,1,0:T(8,128)(2,1)S(1)} collective-permute-done((bf16[2,2,32,1024]{3,2,1,0:T(8,128)(2,1)S(1)}, bf16[2,2,32,1024]{3,2,1,0:T(8,128)(2,1)S(1)}, u32[]{:S(2)}, u32[]{:S(2)}) %collective-permute-start.6) | collective-permute-done | bytes 262176 | tf_op jit(solution)/shard_map/ppermute | solution.py:426
  33.9 1.3 %collective-permute-start.13 = (f32[2,2,32,1024]{3,2,1,0:T(8,128)S(1)}, f32[2,2,32,1024]{3,2,1,0:T(8,128)S(1)}, u32[]{:S(2)}, u32[]{:S(2)}) collective-permute-start(f32[2,2,32,1024]{3,2,1,0:T(8,128)S(1)} %get-tuple-element.87), channel_id=1, source_target_pairs={{0,8},{8,0},{16,24},{24,16},{1,9},{9,1},{17,25},{25,17},{2,10},{10... | collective-permute-start | bytes 1572872 | tf_op jit(solution)/shard_map/ppermute | solution.py:426
  35.2 1.2 %collective-permute-start.14 = (bf16[2,32,1024]{2,1,0:T(8,128)(2,1)S(1)}, bf16[2,32,1024]{2,1,0:T(8,128)(2,1)S(1)}, u32[]{:S(2)}, u32[]{:S(2)}) collective-permute-start(bf16[2,32,1024]{2,1,0:T(8,128)(2,1)S(1)} %get-tuple-element.88), channel_id=1, source_target_pairs={{0,16},{8,24},{16,0},{24,8},{1,17},{9,25},{17,1},{25,9},{2,18},{10... | collective-permute-start | bytes 393224 | tf_op jit(solution)/shard_map/ppermute | solution.py:426
  36.4 0.6 collective-permute-start.18
  36.9 3.1 %collective-permute-done.7.refs_6_ = bf16[2,2,32,1024]{3,2,1,0:T(8,128)(2,1)S(1)} collective-permute-done((bf16[2,2,32,1024]{3,2,1,0:T(8,128)(2,1)S(1)}, bf16[2,2,32,1024]{3,2,1,0:T(8,128)(2,1)S(1)}, u32[]{:S(2)}, u32[]{:S(2)}) %collective-permute-start.7) | collective-permute-done | bytes 262176 | tf_op jit(solution)/shard_map/ppermute | solution.py:426
  40.0 3.8 %columns_0.1 = (f32[2,32,1024]{2,1,0:T(8,128)S(1)}, f32[2,32,1024]{2,1,0:T(8,128)S(1)}, bf16[2,32,1024]{2,1,0:T(8,128)(2,1)S(1)}, bf16[2,32,1024]{2,1,0:T(8,128)(2,1)S(1)}) custom-call(s32[1]{0:T(128)} %bitcast.me_ref.refs_0_, f32[4,2,32,1024]{3,2,1,0:T(8,128)S(1)} %get-tuple-element.59.own_cot, ...), custom_call_target="tpu_custom_call" | custom-call | flops 4000000000 | bytes 3000000 | tf_op jit(solution)/shard_map/columns_0/pallas_call | solution.py:324
  43.8 1.2 %collective-permute-start.9 = (bf16[2,32,1024]{2,1,0:T(8,128)(2,1)S(1)}, bf16[2,32,1024]{2,1,0:T(8,128)(2,1)S(1)}, u32[]{:S(2)}, u32[]{:S(2)}) collective-permute-start(bf16[2,32,1024]{2,1,0:T(8,128)(2,1)S(1)} %get-tuple-element.80), channel_id=1, source_target_pairs={{0,16},{8,24},{16,0},{24,8},{1,17},{9,25},{17,1},{25,9},{2,18},{10... | collective-permute-start | bytes 393224 | tf_op jit(solution)/shard_map/ppermute | solution.py:426
  45.8 3.8 %columns_1.1 = (f32[2,32,1024]{2,1,0:T(8,128)S(1)}, f32[2,32,1024]{2,1,0:T(8,128)S(1)}, bf16[2,32,1024]{2,1,0:T(8,128)(2,1)S(1)}, bf16[2,32,1024]{2,1,0:T(8,128)(2,1)S(1)}) custom-call(s32[1]{0:T(128)} %bitcast.me_ref.refs_0_, f32[4,2,32,1024]{3,2,1,0:T(8,128)S(1)} %get-tuple-element.59.own_cot, ...), custom_call_target="tpu_custom_call" | custom-call | flops 4000000000 | bytes 3000000 | tf_op jit(solution)/shard_map/columns_1/pallas_call | solution.py:324
  49.6 1.2 %collective-permute-start.16 = (bf16[2,32,1024]{2,1,0:T(8,128)(2,1)S(1)}, bf16[2,32,1024]{2,1,0:T(8,128)(2,1)S(1)}, u32[]{:S(2)}, u32[]{:S(2)}) collective-permute-start(bf16[2,32,1024]{2,1,0:T(8,128)(2,1)S(1)} %get-tuple-element.92), channel_id=1, source_target_pairs={{0,16},{8,24},{16,0},{24,8},{1,17},{9,25},{17,1},{25,9},{2,18},{10... | collective-permute-start | bytes 393224 | tf_op jit(solution)/shard_map/ppermute | solution.py:426
  50.8 0.6 collective-permute-start.23
  51.9 1.4 %collective-permute-start.17 = (bf16[2,32,1024]{2,1,0:T(8,128)(2,1)S(1)}, bf16[2,32,1024]{2,1,0:T(8,128)(2,1)S(1)}, u32[]{:S(2)}, u32[]{:S(2)}) collective-permute-start(bf16[2,32,1024]{2,1,0:T(8,128)(2,1)S(1)} %get-tuple-element.93), channel_id=1, source_target_pairs={{0,24},{8,16},{16,8},{24,0},{1,25},{9,17},{17,9},{25,1},{2,26},{10... | collective-permute-start | bytes 393224 | tf_op jit(solution)/shard_map/ppermute | solution.py:426
  53.8 4.0 %collective-permute-start.11 = (bf16[2,32,1024]{2,1,0:T(8,128)(2,1)S(1)}, bf16[2,32,1024]{2,1,0:T(8,128)(2,1)S(1)}, u32[]{:S(2)}, u32[]{:S(2)}) collective-permute-start(bf16[2,32,1024]{2,1,0:T(8,128)(2,1)S(1)} %get-tuple-element.82), channel_id=1, source_target_pairs={{0,1},{1,2},{2,3},{3,4},{4,5},{5,6},{6,7},{8,9},{9,10},{10,11},{11... | collective-permute-start | bytes 393224 | tf_op jit(solution)/shard_map/ppermute | solution.py:433
  57.8 2.4 %collective-permute-start.12 = (bf16[2,32,1024]{2,1,0:T(8,128)(2,1)S(1)}, bf16[2,32,1024]{2,1,0:T(8,128)(2,1)S(1)}, u32[]{:S(2)}, u32[]{:S(2)}) collective-permute-start(bf16[2,32,1024]{2,1,0:T(8,128)(2,1)S(1)} %get-tuple-element.83), channel_id=1, source_target_pairs={{1,0},{2,1},{3,2},{4,3},{5,4},{6,5},{7,6},{9,8},{10,9},{11,10},{12... | collective-permute-start | bytes 393224 | tf_op jit(solution)/shard_map/ppermute | solution.py:433
  60.2 3.8 %columns_2.1 = (f32[2,32,1024]{2,1,0:T(8,128)S(1)}, f32[2,32,1024]{2,1,0:T(8,128)S(1)}, bf16[2,32,1024]{2,1,0:T(8,128)(2,1)S(1)}, bf16[2,32,1024]{2,1,0:T(8,128)(2,1)S(1)}) custom-call(s32[1]{0:T(128)} %bitcast.me_ref.refs_0_, f32[4,2,32,1024]{3,2,1,0:T(8,128)S(1)} %get-tuple-element.59.own_cot, ...), custom_call_target="tpu_custom_call" | custom-call | flops 4000000000 | bytes 3000000 | tf_op jit(solution)/shard_map/columns_2/pallas_call | solution.py:324
  64.0 1.3 %collective-permute-start.20 = (bf16[2,32,1024]{2,1,0:T(8,128)(2,1)S(1)}, bf16[2,32,1024]{2,1,0:T(8,128)(2,1)S(1)}, u32[]{:S(2)}, u32[]{:S(2)}) collective-permute-start(bf16[2,32,1024]{2,1,0:T(8,128)(2,1)S(1)} %get-tuple-element.97), channel_id=1, source_target_pairs={{0,16},{8,24},{16,0},{24,8},{1,17},{9,25},{17,1},{25,9},{2,18},{10... | collective-permute-start | bytes 393224 | tf_op jit(solution)/shard_map/ppermute | solution.py:426
  65.2 1.4 %collective-permute-start.21 = (bf16[2,32,1024]{2,1,0:T(8,128)(2,1)S(1)}, bf16[2,32,1024]{2,1,0:T(8,128)(2,1)S(1)}, u32[]{:S(2)}, u32[]{:S(2)}) collective-permute-start(bf16[2,32,1024]{2,1,0:T(8,128)(2,1)S(1)} %get-tuple-element.98), channel_id=1, source_target_pairs={{0,24},{8,16},{16,8},{24,0},{1,25},{9,17},{17,9},{25,1},{2,26},{10... | collective-permute-start | bytes 393224 | tf_op jit(solution)/shard_map/ppermute | solution.py:426
  67.2 3.8 %columns_3.1 = (f32[2,32,1024]{2,1,0:T(8,128)S(1)}, f32[2,32,1024]{2,1,0:T(8,128)S(1)}, bf16[2,32,1024]{2,1,0:T(8,128)(2,1)S(1)}, bf16[2,32,1024]{2,1,0:T(8,128)(2,1)S(1)}) custom-call(s32[1]{0:T(128)} %bitcast.me_ref.refs_0_, f32[4,2,32,1024]{3,2,1,0:T(8,128)S(1)} %get-tuple-element.59.own_cot, ...), custom_call_target="tpu_custom_call" | custom-call | flops 4000000000 | bytes 3000000 | tf_op jit(solution)/shard_map/columns_3/pallas_call | solution.py:324
  71.1 1.1 %collective-permute-start.25 = (bf16[2,32,1024]{2,1,0:T(8,128)(2,1)S(1)}, bf16[2,32,1024]{2,1,0:T(8,128)(2,1)S(1)}, u32[]{:S(2)}, u32[]{:S(2)}) collective-permute-start(bf16[2,32,1024]{2,1,0:T(8,128)(2,1)S(1)} %get-tuple-element.103), channel_id=1, source_target_pairs={{0,16},{8,24},{16,0},{24,8},{1,17},{9,25},{17,1},{25,9},{2,18},{10... | collective-permute-start | bytes 393224 | tf_op jit(solution)/shard_map/ppermute | solution.py:426
  72.2 1.0 %collective-permute-start.26 = (bf16[2,32,1024]{2,1,0:T(8,128)(2,1)S(1)}, bf16[2,32,1024]{2,1,0:T(8,128)(2,1)S(1)}, u32[]{:S(2)}, u32[]{:S(2)}) collective-permute-start(bf16[2,32,1024]{2,1,0:T(8,128)(2,1)S(1)} %get-tuple-element.104), channel_id=1, source_target_pairs={{0,24},{8,16},{16,8},{24,0},{1,25},{9,17},{17,9},{25,1},{2,26},{10... | collective-permute-start | bytes 393224 | tf_op jit(solution)/shard_map/ppermute | solution.py:426
  73.2 3.6 %final_0.1.refs_20_ = f32[2,32,16,1024]{3,2,1,0:T(8,128)} custom-call(s32[1]{0:T(128)} %bitcast.me_ref.refs_0_, f32[16,32,1024]{2,1,0:T(8,128)S(1)} %get-tuple-element.58.diff_ref.refs_1_, bf16[2,32,1024]{2,1,0:T(8,128)(2,1)S(1)} %collective-permute-done.11.refs_15_.refs_2_, bf16[2,32,1024]{2,1,0:T(8,128)(2,1)S(1)} %collective-permute-done.12.refs_16_.refs_3_, ...), custom_call_target="tpu_custom_call" | custom-call | flops 1 | bytes 1 | tf_op jit(solution)/shard_map/final_0/pallas_call | solution.py:409
  76.9 2.3 %collective-permute-done.26.refs_19_ = bf16[2,32,1024]{2,1,0:T(8,128)(2,1)S(1)} collective-permute-done((bf16[2,32,1024]{2,1,0:T(8,128)(2,1)S(1)}, bf16[2,32,1024]{2,1,0:T(8,128)(2,1)S(1)}, u32[]{:S(2)}, u32[]{:S(2)}) %collective-permute-start.26) | collective-permute-done | bytes 131104 | tf_op jit(solution)/shard_map/ppermute | solution.py:426
  79.2 3.7 %final_1.1 = f32[2,32,16,1024]{3,2,1,0:T(8,128)} custom-call(s32[1]{0:T(128)} %bitcast.me_ref.refs_0_, f32[16,32,1024]{2,1,0:T(8,128)S(1)} %get-tuple-element.58.diff_ref.refs_1_, bf16[2,32,1024]{2,1,0:T(8,128)(2,1)S(1)} %collective-permute-done.11.refs_15_.refs_2_, ...), custom_call_target="tpu_custom_call", output_to_operand_aliasing={{}: (20, {})} | custom-call | flops 1 | bytes 1 | tf_op jit(solution)/shard_map/final_1/pallas_call | solution.py:409
  (42 shorter events, 3.6 us)
Async XLA Ops:
  0.0 15.2 %copy-start.1 = (bf16[1024,256]{1,0:T(8,128)(2,1)S(1)}, bf16[1024,256]{1,0:T(8,128)(2,1)}, u32[]{:S(2)}) copy-start(bf16[1024,256]{1,0:T(8,128)(2,1)} %refs_9_.7) | copy-start | bytes 1572868
  0.0 15.2 %copy-start.2 = (f32[2,128,128]{2,1,0:T(8,128)S(1)}, f32[2,128,128]{2,1,0:T(8,128)}, u32[]{:S(2)}) copy-start(f32[2,128,128]{2,1,0:T(8,128)} %refs_7_.7) | copy-start | bytes 393220
  0.0 15.2 %copy-start = (bf16[256,1024]{1,0:T(8,128)(2,1)S(1)}, bf16[256,1024]{1,0:T(8,128)(2,1)}, u32[]{:S(2)}) copy-start(bf16[256,1024]{1,0:T(8,128)(2,1)} %wout_ref.1) | copy-start | bytes 1572868
  3.4 20.7 %collective-permute-start.1 = (bf16[4,2,32,1024]{3,2,1,0:T(8,128)(2,1)S(1)}, bf16[4,2,32,1024]{3,2,1,0:T(8,128)(2,1)S(1)}, u32[]{:S(2)}, u32[]{:S(2)}) collective-permute-start(bf16[4,2,32,1024]{3,2,1,0:T(8,128)(2,1)S(1)} %get-tuple-element.60), channel_id=1, source_target_pairs={{0,16},{8,24},{16,0},{24,8},{1,17},{9,25},{17,1},{25,9},{2,18},{10... | collective-permute-start | bytes 1572872 | tf_op jit(solution)/shard_map/ppermute | solution.py:426
  4.7 19.4 %collective-permute-start = (bf16[4,2,32,1024]{3,2,1,0:T(8,128)(2,1)S(1)}, bf16[4,2,32,1024]{3,2,1,0:T(8,128)(2,1)S(1)}, u32[]{:S(2)}, u32[]{:S(2)}) collective-permute-start(bf16[4,2,32,1024]{3,2,1,0:T(8,128)(2,1)S(1)} %get-tuple-element.55.after_ref), channel_id=1, source_target_pairs={{0,8},{8,0},{16,24},{24,16},{1,9},{9,1},{17,25},{25,17},{2,10},{10... | collective-permute-start | bytes 1572872 | tf_op jit(solution)/shard_map/ppermute | solution.py:426
  5.7 23.1 %collective-permute-start.2 = (bf16[4,2,32,1024]{3,2,1,0:T(8,128)(2,1)S(1)}, bf16[4,2,32,1024]{3,2,1,0:T(8,128)(2,1)S(1)}, u32[]{:S(2)}, u32[]{:S(2)}) collective-permute-start(bf16[4,2,32,1024]{3,2,1,0:T(8,128)(2,1)S(1)} %get-tuple-element.61), channel_id=1, source_target_pairs={{0,24},{8,16},{16,8},{24,0},{1,25},{9,17},{17,9},{25,1},{2,26},{10... | collective-permute-start | bytes 1572872 | tf_op jit(solution)/shard_map/ppermute | solution.py:426
  9.0 15.1 %collective-permute-start.3 = (bf16[2,32,1024]{2,1,0:T(8,128)(2,1)S(1)}, bf16[2,32,1024]{2,1,0:T(8,128)(2,1)S(1)}, u32[]{:S(2)}, u32[]{:S(2)}) collective-permute-start(bf16[2,32,1024]{2,1,0:T(8,128)(2,1)S(1)} %get-tuple-element.63), channel_id=1, source_target_pairs={{0,1},{1,2},{2,3},{3,4},{4,5},{5,6},{6,7},{8,9},{9,10},{10,11},{11... | collective-permute-start | bytes 393224 | tf_op jit(solution)/shard_map/ppermute | solution.py:433
  12.2 11.9 %collective-permute-start.4 = (bf16[2,32,1024]{2,1,0:T(8,128)(2,1)S(1)}, bf16[2,32,1024]{2,1,0:T(8,128)(2,1)S(1)}, u32[]{:S(2)}, u32[]{:S(2)}) collective-permute-start(bf16[2,32,1024]{2,1,0:T(8,128)(2,1)S(1)} %get-tuple-element.56.after_ref), channel_id=1, source_target_pairs={{1,0},{2,1},{3,2},{4,3},{5,4},{6,5},{7,6},{9,8},{10,9},{11,10},{12... | collective-permute-start | bytes 393224 | tf_op jit(solution)/shard_map/ppermute | solution.py:433
  24.3 15.7 %collective-permute-start.5 = (f32[2,2,32,1024]{3,2,1,0:T(8,128)S(1)}, f32[2,2,32,1024]{3,2,1,0:T(8,128)S(1)}, u32[]{:S(2)}, u32[]{:S(2)}) collective-permute-start(f32[2,2,32,1024]{3,2,1,0:T(8,128)S(1)} %get-tuple-element.68), channel_id=1, source_target_pairs={{0,8},{8,0},{16,24},{24,16},{1,9},{9,1},{17,25},{25,17},{2,10},{10... | collective-permute-start | bytes 1572872 | tf_op jit(solution)/shard_map/ppermute | solution.py:426
  25.5 8.4 %collective-permute-start.6 = (bf16[2,2,32,1024]{3,2,1,0:T(8,128)(2,1)S(1)}, bf16[2,2,32,1024]{3,2,1,0:T(8,128)(2,1)S(1)}, u32[]{:S(2)}, u32[]{:S(2)}) collective-permute-start(bf16[2,2,32,1024]{3,2,1,0:T(8,128)(2,1)S(1)} %get-tuple-element.69), channel_id=1, source_target_pairs={{0,16},{8,24},{16,0},{24,8},{1,17},{9,25},{17,1},{25,9},{2,18},{10... | collective-permute-start | bytes 786440 | tf_op jit(solution)/shard_map/ppermute | solution.py:426
  26.7 13.3 %collective-permute-start.7 = (bf16[2,2,32,1024]{3,2,1,0:T(8,128)(2,1)S(1)}, bf16[2,2,32,1024]{3,2,1,0:T(8,128)(2,1)S(1)}, u32[]{:S(2)}, u32[]{:S(2)}) collective-permute-start(bf16[2,2,32,1024]{3,2,1,0:T(8,128)(2,1)S(1)} %get-tuple-element.70), channel_id=1, source_target_pairs={{0,24},{8,16},{16,8},{24,0},{1,25},{9,17},{17,9},{25,1},{2,26},{10... | collective-permute-start | bytes 786440 | tf_op jit(solution)/shard_map/ppermute | solution.py:426
  33.9 11.9 %collective-permute-start.13 = (f32[2,2,32,1024]{3,2,1,0:T(8,128)S(1)}, f32[2,2,32,1024]{3,2,1,0:T(8,128)S(1)}, u32[]{:S(2)}, u32[]{:S(2)}) collective-permute-start(f32[2,2,32,1024]{3,2,1,0:T(8,128)S(1)} %get-tuple-element.87), channel_id=1, source_target_pairs={{0,8},{8,0},{16,24},{24,16},{1,9},{9,1},{17,25},{25,17},{2,10},{10... | collective-permute-start | bytes 1572872 | tf_op jit(solution)/shard_map/ppermute | solution.py:426
  35.2 10.1 %collective-permute-start.14 = (bf16[2,32,1024]{2,1,0:T(8,128)(2,1)S(1)}, bf16[2,32,1024]{2,1,0:T(8,128)(2,1)S(1)}, u32[]{:S(2)}, u32[]{:S(2)}) collective-permute-start(bf16[2,32,1024]{2,1,0:T(8,128)(2,1)S(1)} %get-tuple-element.88), channel_id=1, source_target_pairs={{0,16},{8,24},{16,0},{24,8},{1,17},{9,25},{17,1},{25,9},{2,18},{10... | collective-permute-start | bytes 393224 | tf_op jit(solution)/shard_map/ppermute | solution.py:426
  36.4 17.4 %collective-permute-start.18 = (bf16[2,32,1024]{2,1,0:T(8,128)(2,1)S(1)}, bf16[2,32,1024]{2,1,0:T(8,128)(2,1)S(1)}, u32[]{:S(2)}, u32[]{:S(2)}) collective-permute-start(bf16[2,32,1024]{2,1,0:T(8,128)(2,1)S(1)} %get-tuple-element.77.refs_12_), channel_id=1, source_target_pairs={{0,24},{8,16},{16,8},{24,0},{1,25},{9,17},{17,9},{25,1},{2,26},{10... | collective-permute-start | bytes 393224 | tf_op jit(solution)/shard_map/ppermute | solution.py:426
  43.8 7.0 %collective-permute-start.9 = (bf16[2,32,1024]{2,1,0:T(8,128)(2,1)S(1)}, bf16[2,32,1024]{2,1,0:T(8,128)(2,1)S(1)}, u32[]{:S(2)}, u32[]{:S(2)}) collective-permute-start(bf16[2,32,1024]{2,1,0:T(8,128)(2,1)S(1)} %get-tuple-element.80), channel_id=1, source_target_pairs={{0,16},{8,24},{16,0},{24,8},{1,17},{9,25},{17,1},{25,9},{2,18},{10... | collective-permute-start | bytes 393224 | tf_op jit(solution)/shard_map/ppermute | solution.py:426
  45.0 6.9 %collective-permute-start.10 = (bf16[2,32,1024]{2,1,0:T(8,128)(2,1)S(1)}, bf16[2,32,1024]{2,1,0:T(8,128)(2,1)S(1)}, u32[]{:S(2)}, u32[]{:S(2)}) collective-permute-start(bf16[2,32,1024]{2,1,0:T(8,128)(2,1)S(1)} %get-tuple-element.81), channel_id=1, source_target_pairs={{0,24},{8,16},{16,8},{24,0},{1,25},{9,17},{17,9},{25,1},{2,26},{10... | collective-permute-start | bytes 393224 | tf_op jit(solution)/shard_map/ppermute | solution.py:426
  45.4 8.0 %collective-permute-start.8 = (f32[2,32,1024]{2,1,0:T(8,128)S(1)}, f32[2,32,1024]{2,1,0:T(8,128)S(1)}, u32[]{:S(2)}, u32[]{:S(2)}) collective-permute-start(f32[2,32,1024]{2,1,0:T(8,128)S(1)} %get-tuple-element.79), channel_id=1, source_target_pairs={{0,8},{8,0},{16,24},{24,16},{1,9},{9,1},{17,25},{25,17},{2,10},{10... | collective-permute-start | bytes 786440 | tf_op jit(solution)/shard_map/ppermute | solution.py:426
  49.6 8.2 %collective-permute-start.16 = (bf16[2,32,1024]{2,1,0:T(8,128)(2,1)S(1)}, bf16[2,32,1024]{2,1,0:T(8,128)(2,1)S(1)}, u32[]{:S(2)}, u32[]{:S(2)}) collective-permute-start(bf16[2,32,1024]{2,1,0:T(8,128)(2,1)S(1)} %get-tuple-element.92), channel_id=1, source_target_pairs={{0,16},{8,24},{16,0},{24,8},{1,17},{9,25},{17,1},{25,9},{2,18},{10... | collective-permute-start | bytes 393224 | tf_op jit(solution)/shard_map/ppermute | solution.py:426
  50.8 15.9 %collective-permute-start.23 = (bf16[2,32,1024]{2,1,0:T(8,128)(2,1)S(1)}, bf16[2,32,1024]{2,1,0:T(8,128)(2,1)S(1)}, u32[]{:S(2)}, u32[]{:S(2)}) collective-permute-start(bf16[2,32,1024]{2,1,0:T(8,128)(2,1)S(1)} %get-tuple-element.89.refs_12_), channel_id=1, source_target_pairs={{0,24},{8,16},{16,8},{24,0},{1,25},{9,17},{17,9},{25,1},{2,26},{10... | collective-permute-start | bytes 393224 | tf_op jit(solution)/shard_map/ppermute | solution.py:426
  51.9 12.0 %collective-permute-start.17 = (bf16[2,32,1024]{2,1,0:T(8,128)(2,1)S(1)}, bf16[2,32,1024]{2,1,0:T(8,128)(2,1)S(1)}, u32[]{:S(2)}, u32[]{:S(2)}) collective-permute-start(bf16[2,32,1024]{2,1,0:T(8,128)(2,1)S(1)} %get-tuple-element.93), channel_id=1, source_target_pairs={{0,24},{8,16},{16,8},{24,0},{1,25},{9,17},{17,9},{25,1},{2,26},{10... | collective-permute-start | bytes 393224 | tf_op jit(solution)/shard_map/ppermute | solution.py:426
  53.4 11.9 %collective-permute-start.22 = (bf16[2,32,1024]{2,1,0:T(8,128)(2,1)S(1)}, bf16[2,32,1024]{2,1,0:T(8,128)(2,1)S(1)}, u32[]{:S(2)}, u32[]{:S(2)}) collective-permute-start(bf16[2,32,1024]{2,1,0:T(8,128)(2,1)S(1)} %get-tuple-element.100), channel_id=1, source_target_pairs={{0,16},{8,24},{16,0},{24,8},{1,17},{9,25},{17,1},{25,9},{2,18},{10... | collective-permute-start | bytes 393224 | tf_op jit(solution)/shard_map/ppermute | solution.py:426
  53.8 12.9 %collective-permute-start.11 = (bf16[2,32,1024]{2,1,0:T(8,128)(2,1)S(1)}, bf16[2,32,1024]{2,1,0:T(8,128)(2,1)S(1)}, u32[]{:S(2)}, u32[]{:S(2)}) collective-permute-start(bf16[2,32,1024]{2,1,0:T(8,128)(2,1)S(1)} %get-tuple-element.82), channel_id=1, source_target_pairs={{0,1},{1,2},{2,3},{3,4},{4,5},{5,6},{6,7},{8,9},{9,10},{10,11},{11... | collective-permute-start | bytes 393224 | tf_op jit(solution)/shard_map/ppermute | solution.py:433
  57.8 9.4 %collective-permute-start.12 = (bf16[2,32,1024]{2,1,0:T(8,128)(2,1)S(1)}, bf16[2,32,1024]{2,1,0:T(8,128)(2,1)S(1)}, u32[]{:S(2)}, u32[]{:S(2)}) collective-permute-start(bf16[2,32,1024]{2,1,0:T(8,128)(2,1)S(1)} %get-tuple-element.83), channel_id=1, source_target_pairs={{1,0},{2,1},{3,2},{4,3},{5,4},{6,5},{7,6},{9,8},{10,9},{11,10},{12... | collective-permute-start | bytes 393224 | tf_op jit(solution)/shard_map/ppermute | solution.py:433
  64.0 7.1 %collective-permute-start.20 = (bf16[2,32,1024]{2,1,0:T(8,128)(2,1)S(1)}, bf16[2,32,1024]{2,1,0:T(8,128)(2,1)S(1)}, u32[]{:S(2)}, u32[]{:S(2)}) collective-permute-start(bf16[2,32,1024]{2,1,0:T(8,128)(2,1)S(1)} %get-tuple-element.97), channel_id=1, source_target_pairs={{0,16},{8,24},{16,0},{24,8},{1,17},{9,25},{17,1},{25,9},{2,18},{10... | collective-permute-start | bytes 393224 | tf_op jit(solution)/shard_map/ppermute | solution.py:426
  65.2 7.0 %collective-permute-start.21 = (bf16[2,32,1024]{2,1,0:T(8,128)(2,1)S(1)}, bf16[2,32,1024]{2,1,0:T(8,128)(2,1)S(1)}, u32[]{:S(2)}, u32[]{:S(2)}) collective-permute-start(bf16[2,32,1024]{2,1,0:T(8,128)(2,1)S(1)} %get-tuple-element.98), channel_id=1, source_target_pairs={{0,24},{8,16},{16,8},{24,0},{1,25},{9,17},{17,9},{25,1},{2,26},{10... | collective-permute-start | bytes 393224 | tf_op jit(solution)/shard_map/ppermute | solution.py:426
  66.7 6.5 %collective-permute-start.19 = (f32[2,32,1024]{2,1,0:T(8,128)S(1)}, f32[2,32,1024]{2,1,0:T(8,128)S(1)}, u32[]{:S(2)}, u32[]{:S(2)}) collective-permute-start(f32[2,32,1024]{2,1,0:T(8,128)S(1)} %get-tuple-element.96), channel_id=1, source_target_pairs={{0,8},{8,0},{16,24},{24,16},{1,9},{9,1},{17,25},{25,17},{2,10},{10... | collective-permute-start | bytes 786440 | tf_op jit(solution)/shard_map/ppermute | solution.py:426
  66.7 6.5 %collective-permute-start.15 = (f32[2,32,1024]{2,1,0:T(8,128)S(1)}, f32[2,32,1024]{2,1,0:T(8,128)S(1)}, u32[]{:S(2)}, u32[]{:S(2)}) collective-permute-start(f32[2,32,1024]{2,1,0:T(8,128)S(1)} %get-tuple-element.91), channel_id=1, source_target_pairs={{0,8},{8,0},{16,24},{24,16},{1,9},{9,1},{17,25},{25,17},{2,10},{10... | collective-permute-start | bytes 786440 | tf_op jit(solution)/shard_map/ppermute | solution.py:426
  71.0 8.2 %collective-permute-start.24 = (f32[2,32,1024]{2,1,0:T(8,128)S(1)}, f32[2,32,1024]{2,1,0:T(8,128)S(1)}, u32[]{:S(2)}, u32[]{:S(2)}) collective-permute-start(f32[2,32,1024]{2,1,0:T(8,128)S(1)} %get-tuple-element.102), channel_id=1, source_target_pairs={{0,8},{8,0},{16,24},{24,16},{1,9},{9,1},{17,25},{25,17},{2,10},{10... | collective-permute-start | bytes 786440 | tf_op jit(solution)/shard_map/ppermute | solution.py:426
  71.1 5.7 %collective-permute-start.25 = (bf16[2,32,1024]{2,1,0:T(8,128)(2,1)S(1)}, bf16[2,32,1024]{2,1,0:T(8,128)(2,1)S(1)}, u32[]{:S(2)}, u32[]{:S(2)}) collective-permute-start(bf16[2,32,1024]{2,1,0:T(8,128)(2,1)S(1)} %get-tuple-element.103), channel_id=1, source_target_pairs={{0,16},{8,24},{16,0},{24,8},{1,17},{9,25},{17,1},{25,9},{2,18},{10... | collective-permute-start | bytes 393224 | tf_op jit(solution)/shard_map/ppermute | solution.py:426
  72.2 6.9 %collective-permute-start.26 = (bf16[2,32,1024]{2,1,0:T(8,128)(2,1)S(1)}, bf16[2,32,1024]{2,1,0:T(8,128)(2,1)S(1)}, u32[]{:S(2)}, u32[]{:S(2)}) collective-permute-start(bf16[2,32,1024]{2,1,0:T(8,128)(2,1)S(1)} %get-tuple-element.104), channel_id=1, source_target_pairs={{0,24},{8,16},{16,8},{24,0},{1,25},{9,17},{17,9},{25,1},{2,26},{10... | collective-permute-start | bytes 393224 | tf_op jit(solution)/shard_map/ppermute | solution.py:426
